TPU v7x, 512 devices: a whole 4x4x16 slice. The times are simulated.
512 devices in a mesh: replica: 4 (over y), context: 16 (over x, z_hi), tensor: 8 (over z_lo, core).
Axes of the slice: x: 4, y: 4, z: 16 (z_hi: 4, z_lo: 4; z = z_hi * 4 + z_lo), core: 2. Of those that a mesh axis runs over, the one named last changes fastest.
Arguments:
- hidden: bfloat16 [4, 2048, 7168], P('replica', 'context', 'tensor'), may hold values from -40 to 40
- q_nope: bfloat16 [4, 2048, 8192], P('replica', 'context', 'tensor'), may hold values from -6 to 6
- q_rope: bfloat16 [4, 2048, 4096], P('replica', 'context', 'tensor'), may hold values from -8 to 8
- w_latent: bfloat16 [7168, 512], P('tensor'), may hold values from -5 to 5
- w_krope: bfloat16 [7168, 64], P('tensor'), may hold values from -0.0625 to 0.0625
- kv_gain: float32 [512], replicated, may hold values from 0.1 to 1.9
- w_uk: bfloat16 [64, 128, 512], P('tensor'), may hold values from -0.5 to 0.5
- w_uv: bfloat16 [64, 512, 128], P('tensor'), may hold values from -1 to 1
- prefix_latent: bfloat16 [4, 1024, 512], P('replica', 'context'), may hold values from -6 to 6
- prefix_rope: bfloat16 [4, 1024, 64], P('replica', 'context'), may hold values from -8 to 8
- prefix_lengths: int32 [4], P('replica'), may hold values from 2 to 1024
- placements: int32 [16, 8], P('context'), may hold values from 0 to 7, each once within a row
Outputs:
- attention: bfloat16 [4, 2048, 8192], P('replica', 'context', 'tensor')
- cache_latent: bfloat16 [4, 32, 32768], P('replica', 'context')
- cache_rope: bfloat16 [4, 32, 4096], P('replica', 'context')
- cache_scale: bfloat16 [4, 32, 256], P('replica', 'context')
Inputs may be any that keep to these rules, and one draw needn't show every extreme that they name: `placements`: each row names every owner slot exactly once.
All inputs are finite; a program needn't handle non-finite values.
Results may differ from a plain program's by a relative error of at most 0.0091.
Values may be sent and summed in bfloat16 or wider, within the bound.
A program may use at most 64 MiB of HBM per device.

v0:
```python
import jax
import jax.numpy as jnp
from jax import lax
from jax.sharding import PartitionSpec as P

BLOCK = 64
TILES = 4


rope_theta = 50000.0
norm_eps = 1e-06
scale_eps = 1e-06
masked_score = -1e30


def rotate(entries, positions):
    half_width = entries.shape[1] // 2
    frequency = rope_theta ** (
        -(jnp.arange(half_width, dtype=jnp.float32) * 2.0) / entries.shape[1]
    )
    angles = positions.astype(jnp.float32)[:, None] * frequency[None, :]
    cosine_part = jnp.cos(angles)
    sine_part = jnp.sin(angles)
    leading = entries[:, :half_width]
    trailing = entries[:, half_width:]
    return jnp.concatenate(
        [
            leading * cosine_part - trailing * sine_part,
            trailing * cosine_part + leading * sine_part,
        ],
        axis=1,
    )


def finish(lat_sum, rope_sum, kv_gain, positions):
    mean_square = jnp.mean(lat_sum * lat_sum, axis=1, keepdims=True)
    key_latent = (lat_sum * lax.rsqrt(mean_square + norm_eps) * kv_gain).astype(jnp.bfloat16)
    return (key_latent, rotate(rope_sum, positions).astype(jnp.bfloat16))


def quantize(key_latent, tile_count):
    row_count = key_latent.shape[0]
    entries = key_latent.astype(jnp.float32).reshape(
        row_count, tile_count, key_latent.shape[1] // tile_count
    )
    tile_scale = (jnp.max(jnp.abs(entries), axis=2) + scale_eps).astype(jnp.bfloat16)
    scale_back = lax.optimization_barrier(tile_scale).astype(jnp.float32)
    stored = (
        (entries / scale_back[:, :, None])
        .astype(jnp.bfloat16)
        .reshape(row_count, key_latent.shape[1])
    )
    return (stored, tile_scale)


def absorb_keys(running, absorbed, query_rope, key_lat, key_rope_part, visible, score_scale):
    row_max, row_sum, weighted = running
    scores = jnp.einsum("qhl,kl->hqk", absorbed, key_lat, preferred_element_type=jnp.float32)
    scores = (
        scores
        + jnp.einsum("qhr,kr->hqk", query_rope, key_rope_part, preferred_element_type=jnp.float32)
    ) * score_scale
    scores = jnp.where(visible[None], scores, masked_score)
    new_max = jnp.maximum(row_max, jnp.max(scores, axis=2))
    rescale = jnp.exp(row_max - new_max)
    exponents = jnp.where(visible[None], jnp.exp(scores - new_max[:, :, None]), 0.0)
    row_sum = row_sum * rescale + jnp.sum(exponents, axis=2)
    weighted = weighted * rescale[:, :, None] + jnp.einsum(
        "hqk,kl->hql", exponents.astype(jnp.bfloat16), key_lat, preferred_element_type=jnp.float32
    )
    return (new_max, row_sum, weighted)


def per_device(
    hidden,
    q_nope,
    q_rope,
    w_latent,
    w_krope,
    kv_gain,
    w_uk,
    w_uv,
    prefix_latent,
    prefix_rope,
    prefix_lengths,
    placements,
):
    tok_rows = hidden.shape[1]
    head_count = w_uk.shape[0]
    nope_width = w_uk.shape[1]
    latent_width = w_uk.shape[2]
    rope_width = w_krope.shape[1]
    value_width = w_uv.shape[2]
    prefix_rows = prefix_latent.shape[1]
    half_rows = tok_rows // 2
    blocks_here = tok_rows // BLOCK
    score_scale = (nope_width + rope_width) ** (-0.5)
    cycle_place = lax.axis_index("context")
    prompt_start = prefix_lengths[0]
    span_start = cycle_place * tok_rows
    lat_term = jnp.dot(hidden[0], w_latent, preferred_element_type=jnp.float32)
    rope_term = jnp.dot(hidden[0], w_krope, preferred_element_type=jnp.float32)
    lat_sum, rope_sum = lax.psum((lat_term, rope_term), "tensor")
    key_latent, key_rope = finish(
        lat_sum,
        rope_sum,
        kv_gain,
        prompt_start + span_start + jnp.arange(tok_rows, dtype=jnp.int32),
    )
    stored, tile_scale = quantize(key_latent, TILES)
    own_blocks = (
        stored.reshape(blocks_here, BLOCK * latent_width),
        key_rope.reshape(blocks_here, BLOCK * rope_width),
        tile_scale.reshape(blocks_here, BLOCK * TILES),
    )
    wanted = lax.axis_index("replica") * blocks_here + jnp.arange(blocks_here, dtype=jnp.int32)
    targets = placements[0]
    selector = (wanted[:, None] == targets[None, :]).astype(jnp.bfloat16)
    cache_latent = jnp.dot(
        selector,
        lax.all_gather(own_blocks[0], "replica", axis=0, tiled=True),
        preferred_element_type=jnp.float32,
    ).astype(jnp.bfloat16)[None]
    cache_rope = jnp.dot(
        selector,
        lax.all_gather(own_blocks[1], "replica", axis=0, tiled=True),
        preferred_element_type=jnp.float32,
    ).astype(jnp.bfloat16)[None]
    cache_scale = jnp.dot(
        selector,
        lax.all_gather(own_blocks[2], "replica", axis=0, tiled=True),
        preferred_element_type=jnp.float32,
    ).astype(jnp.bfloat16)[None]
    nope_rows = q_nope[0]
    rope_rows = q_rope[0]
    query_pos = span_start + jnp.arange(tok_rows, dtype=jnp.int32)
    absorbed = jnp.einsum(
        "thn,hnl->thl",
        nope_rows.reshape(tok_rows, head_count, nope_width),
        w_uk,
        preferred_element_type=jnp.float32,
    ).astype(jnp.bfloat16)
    query_rope = rope_rows.reshape(tok_rows, head_count, rope_width)
    shard_rows = prefix_rows + tok_rows
    local_keys = (
        jnp.concatenate([prefix_latent[0], key_latent], axis=0),
        jnp.concatenate([prefix_rope[0], key_rope], axis=0),
    )
    start_state = (
        jnp.full((head_count, tok_rows), masked_score, jnp.float32),
        jnp.zeros((head_count, tok_rows), jnp.float32),
        jnp.zeros((head_count, tok_rows, latent_width), jnp.float32),
    )
    lat_piece = lax.all_gather(local_keys[0], "context", axis=0, tiled=True)
    rope_piece = lax.all_gather(local_keys[1], "context", axis=0, tiled=True)
    shard_count = lat_piece.shape[0] // shard_rows
    group = 1
    for candidate in range(1, shard_count + 1):
        if shard_count % candidate == 0 and candidate * shard_rows <= 1024:
            group = candidate
    block_rows = group * shard_rows

    def per_block(block_step, running):
        row_offset = block_step * block_rows
        key_lat = lax.dynamic_slice_in_dim(lat_piece, row_offset, block_rows)
        key_rope_part = lax.dynamic_slice_in_dim(rope_piece, row_offset, block_rows)
        local_row = row_offset + jnp.arange(block_rows, dtype=jnp.int32)
        shard_id = local_row // shard_rows
        within = local_row % shard_rows
        is_prefix = within < prefix_rows
        prefix_ok = shard_id * prefix_rows + within < prompt_start
        span_index = shard_id * tok_rows + within - prefix_rows
        visible = jnp.where(
            is_prefix[None, :], prefix_ok[None, :], span_index[None, :] <= query_pos[:, None]
        )
        return lax.cond(
            jnp.any(visible),
            lambda state_in: absorb_keys(
                state_in, absorbed, query_rope, key_lat, key_rope_part, visible, score_scale
            ),
            lambda state_in: state_in,
            running,
        )

    final_state = lax.fori_loop(0, shard_count // group, per_block, start_state)
    latent_out = (final_state[2] / final_state[1][:, :, None]).astype(jnp.bfloat16)
    projected = jnp.einsum(
        "hql,hlv->qhv", latent_out, w_uv, preferred_element_type=jnp.float32
    ).astype(jnp.bfloat16)
    projected = projected.reshape(tok_rows, head_count * value_width)
    first_half = projected[:half_rows]
    second_half = projected[half_rows:]
    attention = jnp.concatenate([first_half, second_half], axis=0)[None]
    return (attention, cache_latent, cache_rope, cache_scale)


def solution(mesh):
    return jax.shard_map(
        per_device,
        mesh=mesh,
        in_specs=(
            P("replica", "context", "tensor"),
            P("replica", "context", "tensor"),
            P("replica", "context", "tensor"),
            P("tensor", None),
            P("tensor", None),
            P(),
            P("tensor", None, None),
            P("tensor", None, None),
            P("replica", "context", None),
            P("replica", "context", None),
            P("replica"),
            P("context", None),
        ),
        out_specs=(
            P("replica", "context", "tensor"),
            P("replica", "context", None),
            P("replica", "context", None),
            P("replica", "context", None),
        ),
        check_vma=False,
    )
```

profile of v0, /device:TPU:7, one launch (start us, length us, event | category | flops | bytes accessed | tf_op | source)
XLA Modules:
  0.0 290.7 jit_solution(4692512290441173006)
XLA Ops:
  7.2 2.4 fusion.33
  11.2 1.2 fusion.31
  12.4 26.5 %psum.15 = f32[128,64]{0,1:T(8,128)S(1)} all-reduce(f32[128,64]{0,1:T(8,128)S(1)} %fusion.31), channel_id=1, replica_groups=mesh['replica'=4,'context'=16,'tensor'=8] {'tensor'}, use_global_device_ids=true, to_apply=%region_2.0 | all-reduce | flops 8192 | bytes 65536 | tf_op jit(solution)/shard_map/psum | solution.py:103
  40.7 47.8 %all-gather = bf16[16,192,64]{1,2,0:T(8,128)(2,1)S(1)} all-gather(bf16[1,192,64]{1,2,0:T(8,128)(2,1)S(1)} %maximum_bitcast_fusion.1), channel_id=1, replica_groups=mesh['replica'=4,'context'=16,'tensor'=8] {'context'}, dimensions={0}, use_global_device_ids=true | all-gather | bytes 417792 | tf_op jit(solution)/shard_map/all_gather | solution.py:155
  88.7 11.3 %all-gather.2 = bf16[4,2,4096]{2,1,0:T(2,128)(2,1)S(1)} all-gather(bf16[1,2,4096]{2,1,0:T(2,128)(2,1)S(1)} %reshape.90), channel_id=1, replica_groups=mesh['replica'=4,'context'=16,'tensor'=8] {'replica'}, dimensions={0}, use_global_device_ids=true | all-gather | bytes 81920 | tf_op jit(solution)/shard_map/all_gather | solution.py:126
  100.4 1.3 reshape.87
  105.7 7.9 %all-gather.3 = bf16[4,2,256]{2,1,0:T(2,128)(2,1)S(1)} all-gather(bf16[1,2,256]{2,1,0:T(2,128)(2,1)S(1)} %reshape.92), channel_id=1, replica_groups=mesh['replica'=4,'context'=16,'tensor'=8] {'replica'}, dimensions={0}, use_global_device_ids=true | all-gather | bytes 5120 | tf_op jit(solution)/shard_map/all_gather | solution.py:131
  115.2 9.9 %all-gather.1 = bf16[4,2,32768]{2,1,0:T(2,128)(2,1)S(1)} all-gather(bf16[1,2,32768]{2,1,0:T(2,128)(2,1)S(1)} %fusion.35), channel_id=1, replica_groups=mesh['replica'=4,'context'=16,'tensor'=8] {'replica'}, dimensions={0}, use_global_device_ids=true | all-gather | bytes 655360 | tf_op jit(solution)/shard_map/all_gather | solution.py:121
  127.0 111.8 %all-gather.6.cloned.1.call-done = bf16[3072,512]{1,0:T(8,128)(2,1)} async-done(((bf16[192,512]{1,0:T(8,128)(2,1)}), bf16[3072,512]{1,0:T(8,128)(2,1)}) %all-gather.6.cloned.1.call-update) | async-done | bytes 3145744 | tf_op jit(solution)/shard_map/all_gather | solution.py:154
  238.8 1.6 broadcast_in_dim.117
  240.4 40.6 %while.20 = (s32[]{:T(128)}, f32[8,128]{1,0:T(8,128)S(1)}, f32[8,128]{1,0:T(8,128)S(1)}, f32[8,128,512]{2,1,0:T(8,128)}, s32[]{:T(128)}, /*index=5*/bf16[3072,51...) while((s32[]{:T(128)}, f32[8,128]{1,0:T(8,128)S(1)}, ...), condition=%wide.region_9.10_spmd.clone, body=%wide.region_3.9_spmd.clone.sunk | while | flops 1720511360 | bytes 52603288 | solution.py:185
  241.1 1.3 fusion.63
  243.1 7.5 %conditional.3 = ((f32[8,128]{1,0:T(8,128)S(1)}, f32[8,128]{1,0:T(8,128)S(1)}, f32[8,128,512]{2,1,0:T(8,128)})) conditional(s32[]{:T(128)} %convert_element_type.122, (f32[8,128]{1,0:T(8,128)S(1)}, f32[8,128]{1,0:T(8,128)S(1)}, f32[8,128,512]{2,1,0:T(8,128)}) %tuple.78, (pred[128,768]{0,1:T(8,128)(4,1)S(1)}, s32[]{:T(128)}, ...), branch_computations={%region_5.5_spmd, %region_6.8_spmd} | conditional | flops 1720190976 | bytes 52494496 | solution.py:176
  243.1 1.6 fusion.12
  247.8 1.4 multiply_add_fusion
  249.2 1.3 copy-done.2
  251.3 1.3 fusion.63
  253.2 7.5 %conditional.3 = ((f32[8,128]{1,0:T(8,128)S(1)}, f32[8,128]{1,0:T(8,128)S(1)}, f32[8,128,512]{2,1,0:T(8,128)})) conditional(s32[]{:T(128)} %convert_element_type.122, (f32[8,128]{1,0:T(8,128)S(1)}, f32[8,128]{1,0:T(8,128)S(1)}, f32[8,128,512]{2,1,0:T(8,128)}) %tuple.78, (pred[128,768]{0,1:T(8,128)(4,1)S(1)}, s32[]{:T(128)}, ...), branch_computations={%region_5.5_spmd, %region_6.8_spmd} | conditional | flops 1720190976 | bytes 52494496 | solution.py:176
  253.3 1.6 fusion.12
  257.9 1.4 multiply_add_fusion
  259.4 1.3 copy-done.2
  261.4 1.3 fusion.63
  263.4 7.5 %conditional.3 = ((f32[8,128]{1,0:T(8,128)S(1)}, f32[8,128]{1,0:T(8,128)S(1)}, f32[8,128,512]{2,1,0:T(8,128)})) conditional(s32[]{:T(128)} %convert_element_type.122, (f32[8,128]{1,0:T(8,128)S(1)}, f32[8,128]{1,0:T(8,128)S(1)}, f32[8,128,512]{2,1,0:T(8,128)}) %tuple.78, (pred[128,768]{0,1:T(8,128)(4,1)S(1)}, s32[]{:T(128)}, ...), branch_computations={%region_5.5_spmd, %region_6.8_spmd} | conditional | flops 1720190976 | bytes 52494496 | solution.py:176
  263.4 1.6 fusion.12
  268.1 1.4 multiply_add_fusion
  269.5 1.3 copy-done.2
  271.5 1.3 fusion.63
  273.5 7.5 %conditional.3 = ((f32[8,128]{1,0:T(8,128)S(1)}, f32[8,128]{1,0:T(8,128)S(1)}, f32[8,128,512]{2,1,0:T(8,128)})) conditional(s32[]{:T(128)} %convert_element_type.122, (f32[8,128]{1,0:T(8,128)S(1)}, f32[8,128]{1,0:T(8,128)S(1)}, f32[8,128,512]{2,1,0:T(8,128)}) %tuple.78, (pred[128,768]{0,1:T(8,128)(4,1)S(1)}, s32[]{:T(128)}, ...), branch_computations={%region_5.5_spmd, %region_6.8_spmd} | conditional | flops 1720190976 | bytes 52494496 | solution.py:176
  273.6 1.6 fusion.12
  278.2 1.4 multiply_add_fusion
  279.7 1.3 copy-done.2
  281.0 2.1 fusion.28
  (106 shorter events, 26.3 us)
Async XLA Ops:
  7.2 33.0 %copy-start = (bf16[8,128,512]{2,1,0:T(8,128)(2,1)S(1)}, bf16[8,128,512]{2,1,0:T(8,128)(2,1)}, u32[]{:S(2)}) copy-start(bf16[8,128,512]{2,1,0:T(8,128)(2,1)} %param.22) | copy-start | bytes 3145732
  7.2 92.8 %copy-start.4 = (bf16[1,128,512]{2,1,0:T(8,128)(2,1)S(1)}, bf16[1,128,512]{2,1,0:T(8,128)(2,1)}, u32[]{:S(2)}) copy-start(bf16[1,128,512]{2,1,0:T(8,128)(2,1)} %param.18) | copy-start | bytes 393220
  7.2 95.9 %all-reduce.2.cloned.1.call-start = ((), (), s32[]{:S(2)}) async-start(), calls=%async_computation | async-start | bytes 524288 | tf_op jit(solution)/shard_map/psum | solution.py:103
  9.7 229.2 %all-gather.6.cloned.1.call-start = ((), (), s32[]{:S(2)}) async-start(), calls=%async_computation.1 | async-start | bytes 3342336 | tf_op jit(solution)/shard_map/all_gather | solution.py:154
  40.7 61.6 %copy-start.7 = (s32[1,8]{1,0:T(1,128)S(1)}, s32[1,8]{1,0:T(1,128)}, u32[]{:S(2)}) copy-start(s32[1,8]{1,0:T(1,128)} %param.27) | copy-start | bytes 100
  40.7 63.5 %copy-start.6 = (f32[512]{0:T(512)S(1)}, f32[512]{0:T(512)}, u32[]{:S(2)}) copy-start(f32[512]{0:T(512)} %param.21) | copy-start | bytes 6148
  100.1 13.7 %copy-start.5 = (bf16[1,64,512]{2,1,0:T(8,128)(2,1)S(1)}, bf16[1,64,512]{2,1,0:T(8,128)(2,1)}, u32[]{:S(2)}) copy-start(bf16[1,64,512]{2,1,0:T(8,128)(2,1)} %param.24) | copy-start | bytes 196612
  238.8 42.2 %copy-start.8 = (bf16[8,512,128]{2,1,0:T(8,128)(2,1)S(1)}, bf16[8,512,128]{2,1,0:T(8,128)(2,1)}, u32[]{:S(2)}) copy-start(bf16[8,512,128]{2,1,0:T(8,128)(2,1)} %param.23) | copy-start | bytes 3145732
  243.1 1.9 copy-start.3
  246.2 1.6 copy-start.1
  249.2 1.3 copy-start.2
  253.3 1.9 copy-start.3
  256.3 1.6 copy-start.1
  259.4 1.3 copy-start.2
  263.4 1.9 copy-start.3
  266.5 1.6 copy-start.1
  269.5 1.3 copy-start.2
  273.5 1.9 copy-start.3
  276.6 1.6 copy-start.1
  279.7 1.3 copy-start.2
Sparse Core Ops, SparseCore 0:
  11.5 85.2 all-reduce.1
  114.7 124.0 all-gather.5
where the time goes:
time: 291 us
  waiting for transfers between devices  112 us (38%)
  blocking collectives  103 us (35%)
  matrix products  25.6 us (9%)
  local copies, waits for them, and re-layouts  17.6 us (6%)
  between operations  15 us (5%)
  other arithmetic  14.5 us (5%)
    all_gather x1, waiting for transfers between devices, per_device(): lat_piece = lax.all_gather(local_keys[0], 'context', axis=0, tiled=True)  112 us
    all_gather x1, blocking collectives, per_device(): rope_piece = lax.all_gather(local_keys[1], 'context', axis=0, tiled=True)  47.8 us
    psum x1, blocking collectives, per_device(): lat_sum, rope_sum = lax.psum((lat_term, rope_term), 'tensor')  26.5 us
    all_gather x1, blocking collectives, per_device(): lax.all_gather(own_blocks[1], 'replica', axis=0, tiled=True)  11.3 us
    cond x28, local copies, waits for them, and re-layouts  10.5 us
    all_gather x1, blocking collectives, per_device(): lax.all_gather(own_blocks[0], 'replica', axis=0, tiled=True)  9.9 us
    all_gather x1, blocking collectives, per_device(): lax.all_gather(own_blocks[2], 'replica', axis=0, tiled=True)  7.86 us
    dot_general x4, matrix products, absorb_keys(): jnp.einsum('qhr,kr->hqk', query_rope, key_rope_part, preferred_element_ty...  6.54 us
  transfers between devices with their start and end apart: 2, of which 1 were waited for; matrix products, arithmetic and copies ran while one was open for 3% of the time, Pallas kernels for 0%

commit v1 on v0

v1 whole, which is shorter than its diff:
```python
import functools
import math

import jax
import jax.numpy as jnp
import numpy as np
from jax import lax
from jax.experimental import pallas as pl
from jax.experimental.pallas import tpu as pltpu
from jax.sharding import PartitionSpec as P

MESH = pl.DeviceIdType.MESH
BLOCK = 64
TILES = 4
PIECE = 16
COLUMNS = 512
ROPE_THETA = 50000.0
NORM_EPS = 1e-06
SCALE_EPS = 1e-06
MASKED = -1e30
FLOOR = -1e29
FAR = 1 << 20


def when(condition, action):
    if isinstance(condition, bool):
        if condition:
            action()
    else:
        pl.when(condition)(action)


def both(*conditions):
    static = [c for c in conditions if isinstance(c, bool)]
    traced = [c for c in conditions if not isinstance(c, bool)]
    if not all(static):
        return False
    if not traced:
        return True
    out = traced[0]
    for c in traced[1:]:
        out = jnp.logical_and(out, c)
    return out


def sine_cosine(angle):
    turns = jnp.floor(angle * np.float32(1.0 / (2.0 * math.pi)) + 0.5)
    high = 6.28125
    middle = float(np.float32(0.0019350051879882812))
    low = 2.0 * math.pi - high - middle
    r = angle - turns * np.float32(high)
    r = r - turns * np.float32(middle)
    r = r - turns * np.float32(low)
    square = r * r
    sine = jnp.full_like(r, 1.0 / math.factorial(17))
    for n in (15, 13, 11, 9, 7, 5, 3, 1):
        sign = -1.0 if (n // 2) % 2 else 1.0
        sine = sine * square + sign / math.factorial(n)
    cosine = jnp.full_like(r, 1.0 / math.factorial(16))
    for n in (14, 12, 10, 8, 6, 4, 2, 0):
        sign = -1.0 if (n // 2) % 2 else 1.0
        cosine = cosine * square + sign / math.factorial(n)
    return sine * r, cosine


def kernel(
    shape,
    length_ref,
    places_ref,
    frequency_ref,
    gain_ref,
    hidden_hbm,
    q_nope_hbm,
    q_rope_hbm,
    w_latent_hbm,
    w_krope_hbm,
    w_uk_hbm,
    w_uv_hbm,
    pre_lat_hbm,
    pre_rope_hbm,
    out_ref,
    cache_lat_ref,
    cache_rope_ref,
    cache_scale_ref,
    hidden,
    q_nope,
    q_rope,
    w_latent,
    w_krope,
    w_uk,
    w_uv,
    pre_lat,
    pre_rope,
    partial,
    partner_part,
    chip_sum,
    group_part,
    keys,
    blocks,
    queries,
    total,
    top,
    weight_sum,
    in_sem,
    ra_send,
    ra_recv,
    rb_send,
    rb_recv,
    px_send,
    px_recv,
    pz_send,
    pz_recv,
    pd_send,
    pd_recv,
    nx_send,
    nx_recv,
    no_send,
    no_recv,
    nz_send,
    nz_recv,
    nd_send,
    nd_recv,
    y_send,
    y_recv,
    yd_send,
    yd_recv,
):
    n_rep, n_x, n_hi, n_lo = shape
    n_z = n_hi * n_lo
    half = n_z // 2
    heads, nope, lat = w_uk.shape
    rope = pre_rope.shape[1]
    width = keys.shape[-1]
    value = w_uv.shape[2]
    tok = hidden.shape[0]

    replica = lax.axis_index("replica")
    context = lax.axis_index("context")
    tensor = lax.axis_index("tensor")
    x = lax.div(context, n_hi)
    z_hi = lax.rem(context, n_hi)
    z_lo = lax.div(tensor, 2)
    core = lax.rem(tensor, 2)
    other = 1 - core
    z = z_hi * n_lo + z_lo
    sign = 1 - 2 * core

    def wrap(place):
        return lax.rem(place + 2 * n_z, n_z)

    def at_z(place):
        return {
            "context": x * n_hi + lax.div(place, n_lo),
            "tensor": lax.rem(place, n_lo) * 2 + core,
        }

    def at_x(place):
        return {"context": place * n_hi + z_hi}

    def x_plus(step):
        return lax.rem(x + step, n_x)

    def r_plus(step):
        return lax.rem(replica + step, n_rep)

    partner = {"tensor": z_lo * 2 + other}
    z_next = at_z(wrap(z + sign))
    z_behind = at_z(wrap(z - sign))

    peers = [z_next, z_behind, partner]
    peers += [at_x(x_plus(d)) for d in range(1, n_x)]
    peers += [{"tensor": lax.rem(z_lo + d, n_lo) * 2 + core} for d in range(1, n_lo)]
    peers += [{"replica": r_plus(d)} for d in range(1, n_rep)]
    barrier = pltpu.get_barrier_semaphore()
    for peer in peers:
        pl.semaphore_signal(barrier, inc=1, device_id=peer, device_id_type=MESH)

    own_pre = pl.multiple_of(z_lo * PIECE, PIECE)
    loads = [
        (hidden_hbm, hidden),
        (w_latent_hbm, w_latent),
        (w_krope_hbm, w_krope),
        (pre_lat_hbm.at[pl.ds(own_pre, PIECE)], pre_lat),
        (pre_rope_hbm.at[pl.ds(own_pre, PIECE)], pre_rope),
        (q_nope_hbm, q_nope),
        (q_rope_hbm, q_rope),
        (w_uk_hbm, w_uk),
        (w_uv_hbm, w_uv),
    ]
    loads = [
        pltpu.make_async_copy(source, target, in_sem.at[i])
        for i, (source, target) in enumerate(loads)
    ]
    for load in loads:
        load.start()

    def send(source, target, send_sem, recv_sem, device):
        return pltpu.make_async_remote_copy(
            src_ref=source,
            dst_ref=target,
            send_sem=send_sem,
            recv_sem=recv_sem,
            device_id=device,
            device_id_type=MESH,
        )

    def same(ref, send_sem, recv_sem, device):
        return send(ref, ref, send_sem, recv_sem, device)

    def ra_copy():
        return send(partial.at[other], partner_part, ra_send, ra_recv, partner)

    def rb_copy(d):
        to = lax.rem(z_lo + d, n_lo)
        return send(
            chip_sum.at[to],
            group_part.at[d - 1],
            rb_send.at[d - 1],
            rb_recv.at[d - 1],
            {"tensor": to * 2 + core},
        )

    def pz_copy(p):
        return same(
            keys.at[0, wrap(z - sign * (p - 1)), x], pz_send.at[p], pz_recv.at[p], z_next
        )

    def pz_arrival(p):
        return same(keys.at[0, wrap(z - sign * p), x], pz_send.at[p], pz_recv.at[p], z_next)

    def px_copy(p, d):
        return same(
            keys.at[0, wrap(z - sign * p), x],
            px_send.at[p, d - 1],
            px_recv.at[p, d - 1],
            at_x(x_plus(d)),
        )

    def px_arrival(p, d):
        return same(
            keys.at[0, wrap(z - sign * p), x_plus(n_x - d)],
            px_send.at[p, d - 1],
            px_recv.at[p, d - 1],
            partner,
        )

    def pd_copy(p):
        return same(keys.at[0, wrap(z - sign * p)], pd_send.at[p], pd_recv.at[p], partner)

    def pd_arrival(p):
        return same(keys.at[0, wrap(z + sign * p)], pd_send.at[p], pd_recv.at[p], partner)

    def prefix_step(p):
        def first():
            pz_arrival(p).wait_recv()
            when(p < half, lambda: pz_copy(p + 1).start())
            for d in range(1, n_x):
                px_copy(p, d).start()

        def second():
            for d in range(1, n_x):
                px_arrival(p - 1, d).wait_recv()
            when(both(p - 1 >= 1, p - 1 < half), lambda: pd_copy(p - 1).start())

        def third():
            pd_arrival(p - 2).wait_recv()

        when(p <= half, first)
        when(p - 1 <= half, second)
        when(both(p - 2 >= 1, p - 2 < half), third)

    own_kind = 1 + core

    def nx_copy(d):
        return same(
            keys.at[own_kind, z, x], nx_send.at[d - 1], nx_recv.at[d - 1], at_x(x_plus(d))
        )

    def nx_arrival(d):
        return same(
            keys.at[own_kind, z, x_plus(n_x - d)],
            nx_send.at[d - 1],
            nx_recv.at[d - 1],
            partner,
        )

    def no_copy():
        return same(keys.at[own_kind, z], no_send, no_recv, partner)

    def no_arrival():
        return same(keys.at[2 - core, z], no_send, no_recv, partner)

    def half_x(who):
        return pl.ds(who * (n_x // 2), n_x // 2)

    def nz_copy(kind, s):
        return same(
            keys.at[kind, wrap(z - sign * (s - 1))],
            nz_send.at[kind - 1, s],
            nz_recv.at[kind - 1, s],
            z_next,
        )

    def nz_arrival(kind, s):
        return same(
            keys.at[kind, wrap(z - sign * s)],
            nz_send.at[kind - 1, s],
            nz_recv.at[kind - 1, s],
            z_next,
        )

    def nz_last_copy(kind):
        return same(
            keys.at[kind, wrap(z - sign * (half - 1)), half_x(core)],
            nz_send.at[kind - 1, half],
            nz_recv.at[kind - 1, half],
            z_next,
        )

    def nz_last_arrival(kind):
        return same(
            keys.at[kind, wrap(z + half), half_x(core)],
            nz_send.at[kind - 1, half],
            nz_recv.at[kind - 1, half],
            z_next,
        )

    def nd_copy(kind, s):
        return same(
            keys.at[kind, wrap(z - sign * s)],
            nd_send.at[kind - 1, s],
            nd_recv.at[kind - 1, s],
            partner,
        )

    def nd_arrival(kind, s):
        return same(
            keys.at[kind, wrap(z + sign * s)],
            nd_send.at[kind - 1, s],
            nd_recv.at[kind - 1, s],
            partner,
        )

    def nd_last_copy(kind):
        return same(
            keys.at[kind, wrap(z + half), half_x(core)],
            nd_send.at[kind - 1, half],
            nd_recv.at[kind - 1, half],
            partner,
        )

    def nd_last_arrival(kind):
        return same(
            keys.at[kind, wrap(z + half), half_x(other)],
            nd_send.at[kind - 1, half],
            nd_recv.at[kind - 1, half],
            partner,
        )

    def new_step(s):
        def middle():
            for kind in (1, 2):
                nz_arrival(kind, s).wait_recv()
                when(s + 1 < half, lambda: nz_copy(kind, s + 1).start())
                when(s + 1 == half, lambda: nz_last_copy(kind).start())
                nd_copy(kind, s).start()

        def last():
            for kind in (1, 2):
                nz_last_arrival(kind).wait_recv()
                nd_last_copy(kind).start()

        when(s < half, middle)
        when(s == half, last)

    def y_copy(d):
        return send(
            keys.at[own_kind, pl.ds(z_hi * n_lo, n_lo), x],
            blocks.at[core, pl.ds(replica * n_lo, n_lo)],
            y_send.at[d - 1],
            y_recv.at[d - 1],
            {"replica": r_plus(d)},
        )

    def y_arrival(d):
        return send(
            keys.at[own_kind, pl.ds(z_hi * n_lo, n_lo), x],
            blocks.at[core, pl.ds(r_plus(n_rep - d) * n_lo, n_lo)],
            y_send.at[d - 1],
            y_recv.at[d - 1],
            partner,
        )

    def yd_copy():
        return same(blocks.at[core], yd_send, yd_recv, partner)

    def yd_arrival():
        return same(blocks.at[other], yd_send, yd_recv, partner)

    loads[0].wait()
    loads[1].wait()
    loads[2].wait()
    lat_term = jnp.dot(hidden[...], w_latent[...], preferred_element_type=jnp.float32)
    rope_term = lax.dot_general(
        hidden[...], w_krope[...], (((1,), (1,)), ((), ())), preferred_element_type=jnp.float32
    )
    rope_term = jnp.concatenate(
        [rope_term, jnp.zeros((tok, width - lat - rope), jnp.float32)], axis=1
    )
    for place in range(n_lo):
        for who in range(2):
            first = (place * 2 + who) * PIECE
            partial[who, place, :, :lat] = lat_term[first : first + PIECE]
            partial[who, place, :, lat:] = rope_term[first : first + PIECE]
    loads[3].wait()
    loads[4].wait()
    keys[0, z, x, :, :lat] = pre_lat[...]
    keys[0, z, x, :, lat:] = jnp.concatenate(
        [pre_rope[...], jnp.zeros((PIECE, width - lat - rope), pre_rope.dtype)], axis=1
    )

    pl.semaphore_wait(barrier, len(peers))
    ra_copy().start()
    pz_copy(1).start()
    for d in range(1, n_x):
        px_copy(0, d).start()

    loads[5].wait()
    loads[6].wait()
    loads[7].wait()
    lanes = lax.broadcasted_iota(jnp.int32, (tok, width - lat), 1)

    def absorb(first, last):
        for head in range(first, last):
            columns = pl.ds(head * tok, tok)
            absorbed = jnp.dot(
                q_nope[:, head * nope : (head + 1) * nope],
                w_uk[head],
                preferred_element_type=jnp.float32,
            )
            queries[:lat, columns] = absorbed.T.astype(jnp.bfloat16)
            pair = q_rope[:, (head // 2) * 2 * rope : (head // 2 + 1) * 2 * rope]
            pair = pair.astype(jnp.float32)
            if head % 2:
                pair = pltpu.roll(pair, rope, 1)
            queries[lat:, columns] = jnp.where(lanes < rope, pair, 0.0).T.astype(jnp.bfloat16)

    absorb(0, heads // 2)

    ra_copy().wait_recv()
    chip_sum[...] = partial[core] + partner_part[...]
    for d in range(1, n_lo):
        rb_copy(d).start()

    if half >= 1:
        prefix_step(1)
    absorb(heads // 2, heads)

    length = length_ref[0]
    position = (
        length
        + context * tok
        + tensor * PIECE
        + lax.broadcasted_iota(jnp.int32, (PIECE, width - lat), 0)
    )
    sine, cosine = sine_cosine(position.astype(jnp.float32) * frequency_ref[...])
    piece_lanes = lax.broadcasted_iota(jnp.int32, (PIECE, width - lat), 1)
    sine = jnp.where(piece_lanes < rope // 2, -sine, sine)
    sine = jnp.where(piece_lanes < rope, sine, 0.0)

    top[...] = jnp.full_like(top, FLOOR)
    weight_sum[...] = jnp.zeros_like(weight_sum)
    total[...] = jnp.zeros_like(total)

    for d in range(1, n_lo):
        rb_copy(d).wait_recv()
    summed = chip_sum[z_lo]
    for d in range(1, n_lo):
        summed = summed + group_part[d - 1]
    lat_sum = summed[:, :lat]
    mean_square = jnp.mean(lat_sum * lat_sum, axis=1, keepdims=True)
    keys[own_kind, z, x, :, :lat] = (
        lat_sum * lax.rsqrt(mean_square + NORM_EPS) * gain_ref[...]
    ).astype(jnp.bfloat16)
    rope_sum = summed[:, lat:]
    swapped = jnp.where(
        piece_lanes < rope // 2,
        pltpu.roll(rope_sum, width - lat - rope // 2, 1),
        pltpu.roll(rope_sum, rope // 2, 1),
    )
    keys[own_kind, z, x, :, lat:] = (rope_sum * cosine + swapped * sine).astype(jnp.bfloat16)

    for d in range(1, n_x):
        nx_copy(d).start()
    prefix_step(2)
    for d in range(1, n_x):
        nx_arrival(d).wait_recv()
    no_copy().start()

    def start_ring(kind):
        if half > 1:
            nz_copy(kind, 1).start()
        else:
            nz_last_copy(kind).start()

    pl.when(core == 0)(lambda: start_ring(1))
    pl.when(core == 1)(lambda: start_ring(2))
    prefix_step(3)
    no_arrival().wait_recv()
    pl.when(core == 1)(lambda: start_ring(1))
    pl.when(core == 0)(lambda: start_ring(2))

    score_scale = float((nope + rope) ** (-0.5) * math.log2(math.e))

    def attend(slots, spread, limit):
        block = n_x * PIECE
        count = len(slots) * block
        row = lax.broadcasted_iota(jnp.int32, (block, tok), 0)
        within = lax.div(row, PIECE) * spread + lax.rem(row, PIECE)
        bias = jnp.concatenate(
            [jnp.where(within <= limit - start, 0.0, MASKED) for _, _, start in slots], axis=0
        )
        key_rows = jnp.concatenate(
            [keys[kind, place].reshape(block, width) for kind, place, _ in slots], axis=0
        )
        latents = key_rows[:, :lat].T
        at_once = min(COLUMNS, heads * tok)
        bias = jnp.concatenate([bias] * (at_once // tok), axis=1)
        for first in range(0, heads * tok, at_once):
            columns = pl.ds(first, at_once)
            scores = jnp.dot(
                key_rows, queries[:, columns], preferred_element_type=jnp.float32
            )
            scores = scores * score_scale + bias
            old_top = top[:, columns]
            new_top = jnp.maximum(old_top, jnp.max(scores, axis=0, keepdims=True))
            top[:, columns] = new_top
            rescale = jnp.exp2(old_top - new_top)
            exponents = jnp.exp2(scores - new_top)
            weight_sum[:, columns] = weight_sum[:, columns] * rescale + jnp.sum(
                exponents, axis=0, keepdims=True
            )
            total[:, columns] = total[:, columns] * rescale + jnp.dot(
                latents, exponents.astype(jnp.bfloat16), preferred_element_type=jnp.float32
            )

    pre_dev = n_lo * PIECE

    def prefix_slot(place):
        return (0, place, lax.div(place, n_lo) * pre_dev + lax.rem(place, n_lo) * PIECE)

    def new_slot(kind, place, push=0):
        start = lax.div(place, n_lo) * tok + lax.rem(place, n_lo) * 2 * PIECE
        return (kind, place, start + (kind - 1) * PIECE + push)

    prefix_limit = length - 1
    new_limit = context * tok + lax.broadcasted_iota(jnp.int32, (n_x * PIECE, tok), 1)

    def iteration(s, carry):
        new_step(s)
        prefix_step(s + 3)

        def from_partner():
            for kind in (1, 2):
                nd_arrival(kind, s - 1).wait_recv()

        pl.when(s > 1)(from_partner)

        def to_owners():
            for place in range(n_lo):
                blocks[core, replica * n_lo + place] = keys[own_kind, z_hi * n_lo + place, x]
            for d in range(1, n_rep):
                y_copy(d).start()

        pl.when(s == n_lo)(to_owners)

        def owners_done():
            for d in range(1, n_rep):
                y_arrival(d).wait_recv()
            yd_copy().start()

        pl.when(s == half)(owners_done)

        def attend_prefix():
            last = jnp.where(s + 1 == half, z, wrap(z - (s + 1)))
            attend(
                [
                    prefix_slot(wrap(z - s)),
                    prefix_slot(wrap(z + s)),
                    prefix_slot(wrap(z + s + 1)),
                    prefix_slot(last),
                ],
                n_hi * pre_dev,
                prefix_limit,
            )

        pl.when(lax.rem(s, 2) == 1)(attend_prefix)
        push = jnp.where(s == 1, FAR, 0)
        before, after = wrap(z - (s - 1)), wrap(z + (s - 1))
        attend(
            [
                new_slot(1, before),
                new_slot(2, before),
                new_slot(1, after, push),
                new_slot(2, after, push),
            ],
            n_hi * tok,
            new_limit,
        )
        return carry

    lax.fori_loop(1, half + 1, iteration, 0)
    for kind in (1, 2):
        nd_last_arrival(kind).wait_recv()
    far = wrap(z + half)
    attend([new_slot(1, far), new_slot(2, far)], n_hi * tok, new_limit)

    loads[8].wait()
    for head in range(heads):
        columns = pl.ds(head * tok, tok)
        latent_out = (total[:, columns] / weight_sum[:, columns]).astype(jnp.bfloat16)
        out_ref[:, head * value : (head + 1) * value] = jnp.dot(
            latent_out.T, w_uv[head], preferred_element_type=jnp.float32
        ).astype(jnp.bfloat16)

    yd_arrival().wait_recv()
    tile = lat // TILES
    per_block = BLOCK // (2 * PIECE)
    stored, ropes, flat_scales = [], [], []
    scale_row = lax.broadcasted_iota(jnp.int32, (BLOCK, BLOCK * TILES), 0)
    scale_lane = lax.broadcasted_iota(jnp.int32, (BLOCK, BLOCK * TILES), 1)
    rope_lane = lax.broadcasted_iota(jnp.int32, (BLOCK, 2 * rope), 1)
    for slot in range(2):
        source = jnp.int32(0)
        for candidate in range(n_rep * 2):
            source = jnp.where(
                places_ref[0, candidate] == replica * 2 + slot, candidate, source
            )
        rows = jnp.concatenate(
            [
                blocks[who, source * per_block + place]
                for place in range(per_block)
                for who in range(2)
            ],
            axis=0,
        ).astype(jnp.float32)
        flat = jnp.zeros((BLOCK, BLOCK * TILES), jnp.float32)
        tiles = []
        for i in range(TILES):
            entries = rows[:, i * tile : (i + 1) * tile]
            scale = jnp.max(jnp.abs(entries), axis=1, keepdims=True) + SCALE_EPS
            scale = scale.astype(jnp.bfloat16).astype(jnp.float32)
            tiles.append(entries / scale)
            flat = jnp.where(scale_lane == scale_row * TILES + i, scale, flat)
        stored.append(jnp.concatenate(tiles, axis=1))
        flat_scales.append(jnp.sum(flat, axis=0, keepdims=True))
        tail = rows[:, lat : lat + 2 * rope]
        following = pltpu.roll(pltpu.roll(tail, BLOCK - 1, 0), rope, 1)
        ropes.append(jnp.where(rope_lane < rope, tail, following))
    for j in range(BLOCK):
        cache_lat_ref[:, j * lat : (j + 1) * lat] = jnp.concatenate(
            [stored[0][j : j + 1], stored[1][j : j + 1]], axis=0
        ).astype(jnp.bfloat16)
    for j in range(BLOCK // 2):
        cache_rope_ref[:, j * 2 * rope : (j + 1) * 2 * rope] = jnp.concatenate(
            [ropes[0][2 * j : 2 * j + 1], ropes[1][2 * j : 2 * j + 1]], axis=0
        ).astype(jnp.bfloat16)
    cache_scale_ref[...] = jnp.concatenate(flat_scales, axis=0).astype(jnp.bfloat16)

    ra_copy().wait_send()
    for d in range(1, n_lo):
        rb_copy(d).wait_send()
    for d in range(1, n_x):
        nx_copy(d).wait_send()
    for d in range(1, n_rep):
        y_copy(d).wait_send()
    no_copy().wait_send()
    yd_copy().wait_send()

    def sent(s, carry):
        pz_copy(s).wait_send()

        def middle():
            pd_copy(s).wait_send()
            for kind in (1, 2):
                nz_copy(kind, s).wait_send()
                nd_copy(kind, s).wait_send()

        def last():
            for kind in (1, 2):
                nz_last_copy(kind).wait_send()
                nd_last_copy(kind).wait_send()

        pl.when(s < half)(middle)
        pl.when(s == half)(last)
        return carry

    lax.fori_loop(1, half + 1, sent, 0)

    def pushed(p, carry):
        for d in range(1, n_x):
            px_copy(p, d).wait_send()
        return carry

    lax.fori_loop(0, half + 1, pushed, 0)


def per_device(
    shape,
    hidden,
    q_nope,
    q_rope,
    w_latent,
    w_krope,
    kv_gain,
    w_uk,
    w_uv,
    prefix_latent,
    prefix_rope,
    prefix_lengths,
    placements,
):
    n_rep, n_x, n_hi, n_lo = shape
    n_z = n_hi * n_lo
    half = n_z // 2
    tok, depth = hidden.shape[1:]
    heads, nope, lat = w_uk.shape
    rope = w_krope.shape[1]
    value = w_uv.shape[2]
    width = -(-(lat + rope) // 128) * 128
    count = rope // 2
    powers = -(np.arange(count, dtype=np.float32) * np.float32(2.0)) / np.float32(rope)
    frequency = np.power(np.float64(ROPE_THETA), powers.astype(np.float64))
    frequency = np.resize(frequency, (1, width - lat)).astype(np.float32)
    vmem = pl.BlockSpec(memory_space=pltpu.VMEM)
    smem = pl.BlockSpec(memory_space=pltpu.SMEM)
    anywhere = pl.BlockSpec(memory_space=pl.ANY)
    bf16, f32 = jnp.bfloat16, jnp.float32
    dma = pltpu.SemaphoreType.DMA
    out = pl.pallas_call(
        functools.partial(kernel, shape),
        out_shape=(
            jax.ShapeDtypeStruct((tok, heads * value), bf16),
            jax.ShapeDtypeStruct((2, BLOCK * lat), bf16),
            jax.ShapeDtypeStruct((2, BLOCK * rope), bf16),
            jax.ShapeDtypeStruct((2, BLOCK * TILES), bf16),
        ),
        in_specs=[smem, smem, vmem, vmem] + [anywhere] * 9,
        out_specs=(vmem, vmem, vmem, vmem),
        scratch_shapes=[
            pltpu.VMEM((tok, depth), bf16),
            pltpu.VMEM((tok, heads * nope), bf16),
            pltpu.VMEM((tok, heads * rope), bf16),
            pltpu.VMEM((depth, lat), bf16),
            pltpu.VMEM((rope, depth), bf16),
            pltpu.VMEM((heads, nope, lat), bf16),
            pltpu.VMEM((heads, lat, value), bf16),
            pltpu.VMEM((PIECE, lat), bf16),
            pltpu.VMEM((PIECE, rope), bf16),
            pltpu.VMEM((2, n_lo, PIECE, width), f32),
            pltpu.VMEM((n_lo, PIECE, width), f32),
            pltpu.VMEM((n_lo, PIECE, width), f32),
            pltpu.VMEM((max(n_lo - 1, 1), PIECE, width), f32),
            pltpu.VMEM((3, n_z, n_x, PIECE, width), bf16),
            pltpu.VMEM((2, n_rep * n_lo, PIECE, width), bf16),
            pltpu.VMEM((width, heads * tok), bf16),
            pltpu.VMEM((lat, heads * tok), f32),
            pltpu.VMEM((1, heads * tok), f32),
            pltpu.VMEM((1, heads * tok), f32),
            dma((9,)),
            dma,
            dma,
            dma((max(n_lo - 1, 1),)),
            dma((max(n_lo - 1, 1),)),
            dma((half + 1, max(n_x - 1, 1))),
            dma((half + 1, max(n_x - 1, 1))),
            dma((half + 1,)),
            dma((half + 1,)),
            dma((half + 1,)),
            dma((half + 1,)),
            dma((max(n_x - 1, 1),)),
            dma((max(n_x - 1, 1),)),
            dma,
            dma,
            dma((2, half + 1)),
            dma((2, half + 1)),
            dma((2, half + 1)),
            dma((2, half + 1)),
            dma((max(n_rep - 1, 1),)),
            dma((max(n_rep - 1, 1),)),
            dma,
            dma,
        ],
        compiler_params=pltpu.CompilerParams(
            collective_id=0, has_side_effects=True, vmem_limit_bytes=56 * 1024 * 1024
        ),
    )(
        prefix_lengths,
        placements,
        jnp.asarray(frequency),
        kv_gain.reshape(1, lat),
        hidden[0],
        q_nope[0],
        q_rope[0],
        w_latent,
        w_krope.T,
        w_uk,
        w_uv,
        prefix_latent[0],
        prefix_rope[0],
    )
    return tuple(result[None] for result in out)


def program(mesh, shape):
    return jax.shard_map(
        functools.partial(per_device, shape),
        mesh=mesh,
        in_specs=(
            P("replica", "context", "tensor"),
            P("replica", "context", "tensor"),
            P("replica", "context", "tensor"),
            P("tensor", None),
            P("tensor", None),
            P(),
            P("tensor", None, None),
            P("tensor", None, None),
            P("replica", "context", None),
            P("replica", "context", None),
            P("replica"),
            P("context", None),
        ),
        out_specs=(
            P("replica", "context", "tensor"),
            P("replica", "context", None),
            P("replica", "context", None),
            P("replica", "context", None),
        ),
        check_vma=False,
    )


def solution(mesh):
    n_hi = 4
    return program(
        mesh,
        (
            mesh.shape["replica"],
            mesh.shape["context"] // n_hi,
            n_hi,
            mesh.shape["tensor"] // 2,
        ),
    )
```

time: 291 us -> 67.4 us (0.23)
  the two profiles are of different devices: /device:TPU:7 before, /device:TPU:1 now
where the time goes in v1:
time: 67.4 us; the launch traced here: 67.2 us
  Pallas kernels  62.2 us (92%)
  local copies, waits for them, and re-layouts  3.67 us (5%)
  between operations  1.3 us (2%)
    pallas_call x1, Pallas kernels, per_device(): pl.pallas_call(functools.partial(kernel, shape), out_shape=(jax.ShapeDtyp...  62.2 us
    unnamed x10, local copies, waits for them, and re-layouts  3.67 us

profile of v1, /device:TPU:1, one launch (start us, length us, event | category | flops | bytes accessed | tf_op | source)
XLA Modules:
  0.0 67.2 jit_solution(9319924064265521882)
XLA Ops:
  1.3 62.2 %shard_map.156 = (bf16[128,1024]{1,0:T(8,128)(2,1)}, bf16[2,32768]{1,0:T(2,128)(2,1)}, bf16[2,4096]{1,0:T(2,128)(2,1)}, bf16[2,256]{1,0:T(2,128)(2,1)}) custom-call(s32[1]{0:T(128)S(6)} %copy.21.length_ref, s32[1,8]{1,0:T(1,128)} %places_ref.1, f32[1,128]{1,0:T(1,128)} %constant.2.clone.frequency_ref, f32[1,512]{1,0:T(1,128)} %bitcast.20, ...), custom_call_target="tpu_custom_call" | custom-call | tf_op jit(solution)/shard_map/pallas_call | solution.py:740
  63.5 0.0 copy-start
  63.5 1.7 %copy.22 = bf16[1,128,1024]{2,1,0:T(8,128)(2,1)} copy(bf16[1,128,1024]{2,1,0:T(8,128)(2,1)} %bitcast.12) | data formatting | bytes 524288
  65.2 0.0 copy-done
  65.2 0.0 copy-start.1
  65.2 0.7 copy.23
  65.9 0.1 copy-done.1
  65.9 0.0 copy-start.2
  65.9 0.6 copy.24
  66.5 0.1 copy-done.2
  66.6 0.6 copy.25
Async XLA Ops:
  63.5 1.7 %copy-start = (bf16[2,32768]{1,0:T(2,128)(2,1)S(1)}, bf16[2,32768]{1,0:T(2,128)(2,1)}, u32[]{:S(2)}) copy-start(bf16[2,32768]{1,0:T(2,128)(2,1)} %get-tuple-element.9) | copy-start | bytes 393220
  65.2 0.7 %copy-start.1 = (bf16[2,4096]{1,0:T(2,128)(2,1)S(1)}, bf16[2,4096]{1,0:T(2,128)(2,1)}, u32[]{:S(2)}) copy-start(bf16[2,4096]{1,0:T(2,128)(2,1)} %get-tuple-element.10) | copy-start | bytes 49156
  65.9 0.7 %copy-start.2 = (bf16[2,256]{1,0:T(2,128)(2,1)S(1)}, bf16[2,256]{1,0:T(2,128)(2,1)}, u32[]{:S(2)}) copy-start(bf16[2,256]{1,0:T(2,128)(2,1)} %get-tuple-element.11) | copy-start | bytes 3076

commit v2 on v1

v2 whole, which is shorter than its diff:
```python
import functools
import math

import jax
import jax.numpy as jnp
import numpy as np
from jax import lax
from jax.experimental import pallas as pl
from jax.experimental.pallas import tpu as pltpu
from jax.sharding import PartitionSpec as P

MESH = pl.DeviceIdType.MESH
BLOCK = 64
TILES = 4
PIECE = 16
ROWS = 256
ROPE_THETA = 50000.0
NORM_EPS = 1e-06
SCALE_EPS = 1e-06
MASKED = -1e30
FLOOR = -1e28


def sine_cosine(angle):
    turns = jnp.floor(angle * np.float32(1.0 / (2.0 * math.pi)) + 0.5)
    high = 6.28125
    middle = float(np.float32(0.0019350051879882812))
    low = 2.0 * math.pi - high - middle
    r = angle - turns * np.float32(high)
    r = r - turns * np.float32(middle)
    r = r - turns * np.float32(low)
    square = r * r
    sine = jnp.full_like(r, 1.0 / math.factorial(17))
    for n in (15, 13, 11, 9, 7, 5, 3, 1):
        sign = -1.0 if (n // 2) % 2 else 1.0
        sine = sine * square + sign / math.factorial(n)
    cosine = jnp.full_like(r, 1.0 / math.factorial(16))
    for n in (14, 12, 10, 8, 6, 4, 2, 0):
        sign = -1.0 if (n // 2) % 2 else 1.0
        cosine = cosine * square + sign / math.factorial(n)
    return sine * r, cosine


def kernel(
    shape,
    length_ref,
    places_ref,
    frequency_ref,
    gain_ref,
    hidden_hbm,
    q_nope_hbm,
    q_rope_hbm,
    w_latent_hbm,
    w_krope_hbm,
    w_uk_hbm,
    w_uv_hbm,
    pre_lat_hbm,
    pre_rope_hbm,
    out_ref,
    cache_lat_ref,
    cache_rope_ref,
    cache_scale_ref,
    hidden,
    q_nope,
    q_rope,
    w_latent,
    w_krope,
    w_uk,
    w_uv,
    pre_lat,
    pre_rope,
    partial,
    partner_part,
    chip_sum,
    group_part,
    keys,
    marks,
    blocks,
    queries,
    total,
    top,
    weight_sum,
    in_sem,
    ra_send,
    ra_recv,
    rb_send,
    rb_recv,
    z1_send,
    z1_recv,
    z2_send,
    z2_recv,
    x_send,
    x_recv,
    xf_send,
    xf_recv,
    d_send,
    d_recv,
    y_send,
    y_recv,
    yd_send,
    yd_recv,
):
    n_rep, n_x, n_hi, n_lo = shape
    n_z = n_hi * n_lo
    heads, nope, lat = w_uk.shape
    rope = pre_rope.shape[1]
    width = keys.shape[-1]
    value = w_uv.shape[2]
    tok = hidden.shape[0]

    replica = lax.axis_index("replica")
    context = lax.axis_index("context")
    tensor = lax.axis_index("tensor")
    x = lax.div(context, n_hi)
    z_hi = lax.rem(context, n_hi)
    z_lo = lax.div(tensor, 2)
    core = lax.rem(tensor, 2)
    other = 1 - core
    z = z_hi * n_lo + z_lo
    own_kind = 1 + core

    def z_plus(step):
        place = lax.rem(z + step + n_z, n_z)
        return {
            "context": x * n_hi + lax.div(place, n_lo),
            "tensor": lax.rem(place, n_lo) * 2 + core,
        }

    def x_place(step):
        return lax.rem(x + step + n_x, n_x)

    def x_plus(step):
        return {"context": x_place(step) * n_hi + z_hi}

    def hi_place(step):
        return lax.rem(z_hi + step, n_hi)

    def r_plus(step):
        return lax.rem(replica + step, n_rep)

    def group(step):
        return lax.rem(z_lo + step + n_lo, n_lo)

    partner = {"tensor": z_lo * 2 + other}
    two = 2 - 4 * lax.rem(z_lo, 2)

    peers = [partner, z_plus(1), z_plus(-1), z_plus(2), z_plus(-2), x_plus(1), x_plus(-1)]
    peers += [{"context": x * n_hi + hi_place(d)} for d in range(1, n_hi)]
    peers += [{"tensor": group(d) * 2 + core} for d in range(1, n_lo)]
    peers += [{"replica": r_plus(d)} for d in range(1, n_rep)]
    barrier = pltpu.get_barrier_semaphore()
    for peer in peers:
        pl.semaphore_signal(barrier, inc=1, device_id=peer, device_id_type=MESH)

    own_pre = pl.multiple_of(z_lo * PIECE, PIECE)
    loads = [
        (hidden_hbm, hidden),
        (w_latent_hbm, w_latent),
        (w_krope_hbm, w_krope),
        (pre_lat_hbm.at[pl.ds(own_pre, PIECE)], pre_lat),
        (pre_rope_hbm.at[pl.ds(own_pre, PIECE)], pre_rope),
        (q_nope_hbm, q_nope),
        (q_rope_hbm, q_rope),
        (w_uk_hbm, w_uk),
        (w_uv_hbm, w_uv),
    ]
    loads = [
        pltpu.make_async_copy(source, target, in_sem.at[i])
        for i, (source, target) in enumerate(loads)
    ]
    for load in loads:
        load.start()

    def send(source, target, send_sem, recv_sem, device):
        return pltpu.make_async_remote_copy(
            src_ref=source,
            dst_ref=target,
            send_sem=send_sem,
            recv_sem=recv_sem,
            device_id=device,
            device_id_type=MESH,
        )

    def same(ref, send_sem, recv_sem, device):
        return send(ref, ref, send_sem, recv_sem, device)

    def ra_copy():
        return send(partial.at[other], partner_part, ra_send, ra_recv, partner)

    def rb_copy(d):
        to = lax.rem(z_lo + d, n_lo)
        return send(
            chip_sum.at[to],
            group_part.at[d - 1],
            rb_send.at[d - 1],
            rb_recv.at[d - 1],
            {"tensor": to * 2 + core},
        )

    def kind_of(flow):
        return own_kind if flow else 0

    def z1_copy(flow, d):
        return same(
            keys.at[kind_of(flow), z_lo, z_hi, x],
            z1_send.at[flow, d - 1],
            z1_recv.at[flow, d - 1],
            {"context": x * n_hi + hi_place(d)},
        )

    def z1_arrival(flow, d):
        return same(
            keys.at[kind_of(flow), z_lo, hi_place(n_hi - d), x],
            z1_send.at[flow, d - 1],
            z1_recv.at[flow, d - 1],
            partner,
        )

    z2_steps = (1, -1, two)

    def z2_copy(flow, i):
        return same(
            keys.at[kind_of(flow), z_lo, :, x],
            z2_send.at[flow, i],
            z2_recv.at[flow, i],
            z_plus(z2_steps[i]),
        )

    def z2_arrival(flow, i):
        return same(
            keys.at[kind_of(flow), group(-z2_steps[i]), :, x],
            z2_send.at[flow, i],
            z2_recv.at[flow, i],
            partner,
        )

    def x_copy(flow, g, i):
        return same(
            keys.at[kind_of(flow), g, :, x],
            x_send.at[flow, g, i],
            x_recv.at[flow, g, i],
            x_plus(1 - 2 * i),
        )

    def x_arrival(flow, g, i):
        return same(
            keys.at[kind_of(flow), g, :, x_place(2 * i - 1)],
            x_send.at[flow, g, i],
            x_recv.at[flow, g, i],
            partner,
        )

    def xf_copy(flow, g):
        way = 1 - 2 * lax.rem(g, 2)
        return same(
            keys.at[kind_of(flow), g, :, x_place(-way)],
            xf_send.at[flow, g],
            xf_recv.at[flow, g],
            x_plus(way),
        )

    def xf_arrival(flow, g):
        return same(
            keys.at[kind_of(flow), g, :, x_place(2)],
            xf_send.at[flow, g],
            xf_recv.at[flow, g],
            partner,
        )

    def d_copy(flow, g):
        return same(
            keys.at[kind_of(flow), g], d_send.at[flow, g], d_recv.at[flow, g], partner
        )

    def d_arrival(flow, g):
        kind = 2 - core if flow else 0
        return same(keys.at[kind, g], d_send.at[flow, g], d_recv.at[flow, g], partner)

    def push_x(flow, g):
        for i in range(2):
            x_copy(flow, g, i).start()

    def forward_x(flow, g):
        for i in range(2):
            x_arrival(flow, g, i).wait_recv()
        xf_copy(flow, g).start()

    def to_partner(flow, g):
        xf_arrival(flow, g).wait_recv()
        d_copy(flow, g).start()

    match = lax.rem(z_lo, 2) == core
    first_group = jnp.where(match, z_lo, group(-1))

    def mine(i):
        return lax.rem(first_group + 2 * i, n_lo)

    def y_copy(d):
        return send(
            keys.at[own_kind, :, z_hi, x],
            blocks.at[core, pl.ds(replica * n_lo, n_lo)],
            y_send.at[d - 1],
            y_recv.at[d - 1],
            {"replica": r_plus(d)},
        )

    def y_arrival(d):
        return send(
            keys.at[own_kind, :, z_hi, x],
            blocks.at[core, pl.ds(r_plus(n_rep - d) * n_lo, n_lo)],
            y_send.at[d - 1],
            y_recv.at[d - 1],
            partner,
        )

    def yd_copy():
        return same(blocks.at[core], yd_send, yd_recv, partner)

    def yd_arrival():
        return same(blocks.at[other], yd_send, yd_recv, partner)

    loads[0].wait()
    loads[1].wait()
    loads[2].wait()
    lat_term = jnp.dot(hidden[...], w_latent[...], preferred_element_type=jnp.float32)
    rope_term = lax.dot_general(
        hidden[...], w_krope[...], (((1,), (1,)), ((), ())), preferred_element_type=jnp.float32
    )
    rope_term = jnp.concatenate(
        [rope_term, jnp.zeros((tok, width - lat - rope), jnp.float32)], axis=1
    )
    for place in range(n_lo):
        for who in range(2):
            first = (place * 2 + who) * PIECE
            partial[who, place, :, :lat] = lat_term[first : first + PIECE]
            partial[who, place, :, lat:] = rope_term[first : first + PIECE]
    loads[3].wait()
    loads[4].wait()
    keys[0, z_lo, z_hi, x, :, :lat] = pre_lat[...]
    length = length_ref[0]
    n_context = n_x * n_hi
    piece_row = lax.broadcasted_iota(jnp.int32, (PIECE, width - lat), 0)
    piece_lanes = lax.broadcasted_iota(jnp.int32, (PIECE, width - lat), 1)
    pre_place = context * (n_lo * PIECE) + z_lo * PIECE + piece_row
    hidden_key = jnp.logical_and(piece_lanes == rope + n_context, pre_place >= length)
    pre_tail = jnp.concatenate(
        [
            pre_rope[...].astype(jnp.float32),
            jnp.zeros((PIECE, width - lat - rope), jnp.float32),
        ],
        axis=1,
    )
    keys[0, z_lo, z_hi, x, :, lat:] = jnp.where(hidden_key, MASKED, pre_tail).astype(
        jnp.bfloat16
    )

    pl.semaphore_wait(barrier, len(peers))
    ra_copy().start()

    def prefix_z1():
        for d in range(1, n_hi):
            z1_copy(0, d).start()

    pl.when(match)(prefix_z1)

    loads[5].wait()
    loads[6].wait()
    loads[7].wait()
    lanes = lax.broadcasted_iota(jnp.int32, (tok, width - lat), 1)
    later = jnp.logical_and(lanes > rope + context, lanes < rope + n_context)
    masks = jnp.where(later, MASKED, jnp.where(lanes == rope + n_context, 1.0, 0.0))
    query_row = lax.broadcasted_iota(jnp.int32, (tok, tok), 0)
    key_lane = lax.broadcasted_iota(jnp.int32, (tok, tok), 1)
    triangle = jnp.where(key_lane > query_row, MASKED, 0.0).astype(jnp.bfloat16)
    marks[...] = jnp.zeros_like(marks)
    mark_row = lax.broadcasted_iota(jnp.int32, (PIECE, tok), 0)
    mark_lane = lax.broadcasted_iota(jnp.int32, (PIECE, tok), 1)
    for place in range(n_lo):
        for who in range(2):
            first = (place * 2 + who) * PIECE
            marks[1 + who, place, z_hi, x] = jnp.where(
                mark_lane == first + mark_row, 1.0, 0.0
            ).astype(jnp.bfloat16)

    def absorb(first, last):
        for head in range(first, last):
            rows = pl.ds(head * tok, tok)
            queries[rows, :lat] = jnp.dot(
                q_nope[:, head * nope : (head + 1) * nope],
                w_uk[head],
                preferred_element_type=jnp.float32,
            ).astype(jnp.bfloat16)
            pair = q_rope[:, (head // 2) * 2 * rope : (head // 2 + 1) * 2 * rope]
            pair = pair.astype(jnp.float32)
            if head % 2:
                pair = pltpu.roll(pair, rope, 1)
            queries[rows, lat:width] = jnp.where(lanes < rope, pair, masks).astype(jnp.bfloat16)
            queries[rows, width:] = triangle

    absorb(0, heads // 2)

    ra_copy().wait_recv()
    chip_sum[...] = partial[core] + partner_part[...]
    for d in range(1, n_lo):
        rb_copy(d).start()

    def prefix_z2():
        for d in range(1, n_hi):
            z1_arrival(0, d).wait_recv()
        for i in range(3):
            z2_copy(0, i).start()
        push_x(0, z_lo)

    pl.when(match)(prefix_z2)
    absorb(heads // 2, heads)

    position = (
        length
        + context * tok
        + tensor * PIECE
        + piece_row
    )
    sine, cosine = sine_cosine(position.astype(jnp.float32) * frequency_ref[...])
    sine = jnp.where(piece_lanes < rope // 2, -sine, sine)
    sine = jnp.where(piece_lanes < rope, sine, 0.0)

    top[...] = jnp.full_like(top, FLOOR)
    weight_sum[...] = jnp.zeros_like(weight_sum)
    total[...] = jnp.zeros_like(total)

    def prefix_far():
        z2_arrival(0, 2).wait_recv()
        push_x(0, group(2))

    def prefix_near():
        for i in (0, 1):
            z2_arrival(0, i).wait_recv()
            push_x(0, group(-z2_steps[i]))

    pl.when(match)(prefix_far)
    pl.when(jnp.logical_not(match))(prefix_near)

    for d in range(1, n_lo):
        rb_copy(d).wait_recv()
    summed = chip_sum[z_lo]
    for d in range(1, n_lo):
        summed = summed + group_part[d - 1]
    lat_sum = summed[:, :lat]
    mean_square = jnp.mean(lat_sum * lat_sum, axis=1, keepdims=True)
    keys[own_kind, z_lo, z_hi, x, :, :lat] = (
        lat_sum * lax.rsqrt(mean_square + NORM_EPS) * gain_ref[...]
    ).astype(jnp.bfloat16)
    rope_sum = summed[:, lat:]
    swapped = jnp.where(
        piece_lanes < rope // 2,
        pltpu.roll(rope_sum, width - lat - rope // 2, 1),
        pltpu.roll(rope_sum, rope // 2, 1),
    )
    new_tail = rope_sum * cosine + swapped * sine
    keys[own_kind, z_lo, z_hi, x, :, lat:] = jnp.where(
        piece_lanes == rope + context, 1.0, new_tail
    ).astype(jnp.bfloat16)

    for d in range(1, n_hi):
        z1_copy(1, d).start()
    for i in range(2):
        forward_x(0, mine(i))
    for d in range(1, n_hi):
        z1_arrival(1, d).wait_recv()
    for i in range(3):
        z2_copy(1, i).start()
    push_x(1, z_lo)
    for i in range(2):
        to_partner(0, mine(i))

    score_scale = float((nope + rope) ** (-0.5) * math.log2(math.e))

    key_count = n_hi * n_x * PIECE

    def attend(places, first):
        key_rows = jnp.concatenate(
            [
                jnp.concatenate(
                    [
                        keys[kind, g].reshape(key_count, width),
                        marks[kind, g].reshape(key_count, tok),
                    ],
                    axis=1,
                )
                for kind, g in places
            ],
            axis=0,
        )
        tiles = len(places) * key_count // 128
        at_once = min(ROWS, heads * tok // 2)
        for part in range(heads * tok // 2 // at_once):
            rows = pl.ds(pl.multiple_of(first + part * at_once, at_once), at_once)
            scores = lax.dot_general(
                queries[rows, :],
                key_rows,
                (((1,), (1,)), ((), ())),
                preferred_element_type=jnp.float32,
            )
            scores = scores * score_scale
            old_top = top[rows, :]
            new_top = jnp.maximum(old_top, jnp.max(scores, axis=1, keepdims=True))
            top[rows, :] = new_top
            rescale = jnp.exp2(old_top - new_top)
            exponents = [
                jnp.exp2(scores[:, i * 128 : (i + 1) * 128] - new_top) for i in range(tiles)
            ]
            weight_sum[rows, :] = weight_sum[rows, :] * rescale + sum(exponents)
            weights = jnp.concatenate([e.astype(jnp.bfloat16) for e in exponents], axis=1)
            total[rows, :] = total[rows, :] * jnp.concatenate(
                [rescale] * (lat // 128), axis=1
            ) + jnp.dot(weights, key_rows[:, :lat], preferred_element_type=jnp.float32)


    def new_group(i):
        step = jnp.where(i == 1, n_lo - 1, jnp.where(i == 2, 1, jnp.where(i == 3, 2, 0)))
        return lax.rem(z_lo + step, n_lo)

    def second_level():
        for i in range(3):
            z2_arrival(1, i).wait_recv()
            push_x(1, group(-z2_steps[i]))
        for d in range(1, n_rep):
            y_copy(d).start()
        for place in range(n_lo):
            blocks[core, replica * n_lo + place] = keys[own_kind, place, z_hi, x]

    def owners():
        for d in range(1, n_rep):
            y_arrival(d).wait_recv()
        yd_copy().start()

    def step_1():
        forward_x(1, group(0))

    def step_2():
        for i in (1, 3):
            d_arrival(0, lax.rem(first_group + i, n_lo)).wait_recv()
        second_level()

    def step_3():
        to_partner(1, group(0))

    def step_4():
        forward_x(1, group(-1))
        d_arrival(1, group(0)).wait_recv()

    def step_5():
        forward_x(1, group(1))
        to_partner(1, group(-1))

    def step_6():
        forward_x(1, group(2))
        to_partner(1, group(1))
        d_arrival(1, group(-1)).wait_recv()

    def step_7():
        to_partner(1, group(2))
        owners()

    def step_8():
        d_arrival(1, group(1)).wait_recv()

    def step_10():
        d_arrival(1, group(2)).wait_recv()

    actions = {
        1: step_1,
        2: step_2,
        3: step_3,
        4: step_4,
        5: step_5,
        6: step_6,
        7: step_7,
        8: step_8,
        10: step_10,
    }

    def iteration(step, carry):
        for number, action in actions.items():
            pl.when(step == number)(action)
        chunk = lax.div(step, 2)
        is_new = chunk >= 2
        g = new_group(jnp.maximum(chunk - 2, 0))
        pre = lax.rem(first_group + chunk, n_lo)
        attend(
            [
                (jnp.where(is_new, 1, 0), jnp.where(is_new, g, pre)),
                (jnp.where(is_new, 2, 0), jnp.where(is_new, g, lax.rem(pre + 2, n_lo))),
            ],
            lax.rem(step, 2) * (heads * tok // 2),
        )
        return carry

    lax.fori_loop(0, 2 * (2 + n_lo), iteration, 0)

    loads[8].wait()
    for head in range(heads):
        rows = pl.ds(head * tok, tok)
        row_sum = jnp.sum(weight_sum[rows, :], axis=1, keepdims=True)
        latent_out = (total[rows, :] / row_sum).astype(jnp.bfloat16)
        out_ref[:, head * value : (head + 1) * value] = jnp.dot(
            latent_out, w_uv[head], preferred_element_type=jnp.float32
        ).astype(jnp.bfloat16)

    yd_arrival().wait_recv()
    tile = lat // TILES
    per_block = BLOCK // (2 * PIECE)
    stored, ropes, flat_scales = [], [], []
    scale_row = lax.broadcasted_iota(jnp.int32, (BLOCK, BLOCK * TILES), 0)
    scale_lane = lax.broadcasted_iota(jnp.int32, (BLOCK, BLOCK * TILES), 1)
    rope_lane = lax.broadcasted_iota(jnp.int32, (BLOCK, 2 * rope), 1)
    for slot in range(2):
        source = jnp.int32(0)
        for candidate in range(n_rep * 2):
            source = jnp.where(
                places_ref[0, candidate] == replica * 2 + slot, candidate, source
            )
        rows = jnp.concatenate(
            [
                blocks[who, source * per_block + place]
                for place in range(per_block)
                for who in range(2)
            ],
            axis=0,
        ).astype(jnp.float32)
        flat = jnp.zeros((BLOCK, BLOCK * TILES), jnp.float32)
        tiles = []
        for i in range(TILES):
            entries = rows[:, i * tile : (i + 1) * tile]
            scale = jnp.max(jnp.abs(entries), axis=1, keepdims=True) + SCALE_EPS
            scale = scale.astype(jnp.bfloat16).astype(jnp.float32)
            tiles.append(entries / scale)
            flat = jnp.where(scale_lane == scale_row * TILES + i, scale, flat)
        stored.append(jnp.concatenate(tiles, axis=1))
        flat_scales.append(jnp.sum(flat, axis=0, keepdims=True))
        tail = rows[:, lat : lat + 2 * rope]
        following = pltpu.roll(pltpu.roll(tail, BLOCK - 1, 0), rope, 1)
        ropes.append(jnp.where(rope_lane < rope, tail, following))
    for j in range(BLOCK):
        cache_lat_ref[:, j * lat : (j + 1) * lat] = jnp.concatenate(
            [stored[0][j : j + 1], stored[1][j : j + 1]], axis=0
        ).astype(jnp.bfloat16)
    for j in range(BLOCK // 2):
        cache_rope_ref[:, j * 2 * rope : (j + 1) * 2 * rope] = jnp.concatenate(
            [ropes[0][2 * j : 2 * j + 1], ropes[1][2 * j : 2 * j + 1]], axis=0
        ).astype(jnp.bfloat16)
    cache_scale_ref[...] = jnp.concatenate(flat_scales, axis=0).astype(jnp.bfloat16)

    ra_copy().wait_send()
    for d in range(1, n_lo):
        rb_copy(d).wait_send()
    for d in range(1, n_rep):
        y_copy(d).wait_send()
    yd_copy().wait_send()

    def z_sent(flow):
        for d in range(1, n_hi):
            z1_copy(flow, d).wait_send()
        for i in range(3):
            z2_copy(flow, i).wait_send()

    def x_sent(flow, g):
        for i in range(2):
            x_copy(flow, g, i).wait_send()
        xf_copy(flow, g).wait_send()
        d_copy(flow, g).wait_send()

    pl.when(match)(lambda: z_sent(0))
    z_sent(1)
    for i in range(2):
        x_sent(0, mine(i))
    for g in range(n_lo):
        x_sent(1, g)


def per_device(
    shape,
    hidden,
    q_nope,
    q_rope,
    w_latent,
    w_krope,
    kv_gain,
    w_uk,
    w_uv,
    prefix_latent,
    prefix_rope,
    prefix_lengths,
    placements,
):
    n_rep, n_x, n_hi, n_lo = shape
    tok, depth = hidden.shape[1:]
    heads, nope, lat = w_uk.shape
    rope = w_krope.shape[1]
    value = w_uv.shape[2]
    width = -(-(lat + rope) // 128) * 128
    count = rope // 2
    powers = -(np.arange(count, dtype=np.float32) * np.float32(2.0)) / np.float32(rope)
    frequency = np.power(np.float64(ROPE_THETA), powers.astype(np.float64))
    frequency = np.resize(frequency, (1, width - lat)).astype(np.float32)
    vmem = pl.BlockSpec(memory_space=pltpu.VMEM)
    smem = pl.BlockSpec(memory_space=pltpu.SMEM)
    anywhere = pl.BlockSpec(memory_space=pl.ANY)
    bf16, f32 = jnp.bfloat16, jnp.float32
    dma = pltpu.SemaphoreType.DMA
    out = pl.pallas_call(
        functools.partial(kernel, shape),
        out_shape=(
            jax.ShapeDtypeStruct((tok, heads * value), bf16),
            jax.ShapeDtypeStruct((2, BLOCK * lat), bf16),
            jax.ShapeDtypeStruct((2, BLOCK * rope), bf16),
            jax.ShapeDtypeStruct((2, BLOCK * TILES), bf16),
        ),
        in_specs=[smem, smem, vmem, vmem] + [anywhere] * 9,
        out_specs=(vmem, vmem, vmem, vmem),
        scratch_shapes=[
            pltpu.VMEM((tok, depth), bf16),
            pltpu.VMEM((tok, heads * nope), bf16),
            pltpu.VMEM((tok, heads * rope), bf16),
            pltpu.VMEM((depth, lat), bf16),
            pltpu.VMEM((rope, depth), bf16),
            pltpu.VMEM((heads, nope, lat), bf16),
            pltpu.VMEM((heads, lat, value), bf16),
            pltpu.VMEM((PIECE, lat), bf16),
            pltpu.VMEM((PIECE, rope), bf16),
            pltpu.VMEM((2, n_lo, PIECE, width), f32),
            pltpu.VMEM((n_lo, PIECE, width), f32),
            pltpu.VMEM((n_lo, PIECE, width), f32),
            pltpu.VMEM((max(n_lo - 1, 1), PIECE, width), f32),
            pltpu.VMEM((3, n_lo, n_hi, n_x, PIECE, width), bf16),
            pltpu.VMEM((3, n_lo, n_hi, n_x, PIECE, tok), bf16),
            pltpu.VMEM((2, n_rep * n_lo, PIECE, width), bf16),
            pltpu.VMEM((heads * tok, width + tok), bf16),
            pltpu.VMEM((heads * tok, lat), f32),
            pltpu.VMEM((heads * tok, 128), f32),
            pltpu.VMEM((heads * tok, 128), f32),
            dma((9,)),
            dma,
            dma,
            dma((max(n_lo - 1, 1),)),
            dma((max(n_lo - 1, 1),)),
            dma((2, n_hi - 1)),
            dma((2, n_hi - 1)),
            dma((2, 3)),
            dma((2, 3)),
            dma((2, n_lo, 2)),
            dma((2, n_lo, 2)),
            dma((2, n_lo)),
            dma((2, n_lo)),
            dma((2, n_lo)),
            dma((2, n_lo)),
            dma((max(n_rep - 1, 1),)),
            dma((max(n_rep - 1, 1),)),
            dma,
            dma,
        ],
        compiler_params=pltpu.CompilerParams(
            collective_id=0, has_side_effects=True, vmem_limit_bytes=56 * 1024 * 1024
        ),
    )(
        prefix_lengths,
        placements,
        jnp.asarray(frequency),
        kv_gain.reshape(1, lat),
        hidden[0],
        q_nope[0],
        q_rope[0],
        w_latent,
        w_krope.T,
        w_uk,
        w_uv,
        prefix_latent[0],
        prefix_rope[0],
    )
    return tuple(result[None] for result in out)


def program(mesh, shape):
    return jax.shard_map(
        functools.partial(per_device, shape),
        mesh=mesh,
        in_specs=(
            P("replica", "context", "tensor"),
            P("replica", "context", "tensor"),
            P("replica", "context", "tensor"),
            P("tensor", None),
            P("tensor", None),
            P(),
            P("tensor", None, None),
            P("tensor", None, None),
            P("replica", "context", None),
            P("replica", "context", None),
            P("replica"),
            P("context", None),
        ),
        out_specs=(
            P("replica", "context", "tensor"),
            P("replica", "context", None),
            P("replica", "context", None),
            P("replica", "context", None),
        ),
        check_vma=False,
    )


def solution(mesh):
    n_hi = 4
    return program(
        mesh,
        (
            mesh.shape["replica"],
            mesh.shape["context"] // n_hi,
            n_hi,
            mesh.shape["tensor"] // 2,
        ),
    )
```

time: 67.4 us -> 70.5 us (1.046)
  the two profiles are of different devices: /device:TPU:1 before, /device:TPU:16 now
where the time goes in v2:
time: 70.5 us; the launch traced here: 70.2 us
  Pallas kernels  65.3 us (93%)
  local copies, waits for them, and re-layouts  3.67 us (5%)
  between operations  1.3 us (2%)
    pallas_call x1, Pallas kernels, per_device(): pl.pallas_call(functools.partial(kernel, shape), out_shape=(jax.ShapeDtyp...  65.3 us
    unnamed x10, local copies, waits for them, and re-layouts  3.67 us

profile of v2, /device:TPU:16, one launch (start us, length us, event | category | flops | bytes accessed | tf_op | source)
XLA Modules:
  0.0 70.2 jit_solution(12386466247192476483)
XLA Ops:
  1.3 65.3 %shard_map.156 = (bf16[128,1024]{1,0:T(8,128)(2,1)}, bf16[2,32768]{1,0:T(2,128)(2,1)}, bf16[2,4096]{1,0:T(2,128)(2,1)}, bf16[2,256]{1,0:T(2,128)(2,1)}) custom-call(s32[1]{0:T(128)S(6)} %copy.21.length_ref, s32[1,8]{1,0:T(1,128)} %places_ref.1, f32[1,128]{1,0:T(1,128)} %constant.2.clone.frequency_ref, f32[1,512]{1,0:T(1,128)} %bitcast.20, ...), custom_call_target="tpu_custom_call" | custom-call | tf_op jit(solution)/shard_map/pallas_call | solution.py:711
  66.6 0.0 copy-start
  66.6 1.7 %copy.22 = bf16[1,128,1024]{2,1,0:T(8,128)(2,1)} copy(bf16[1,128,1024]{2,1,0:T(8,128)(2,1)} %bitcast.12) | data formatting | bytes 524288
  68.3 0.0 copy-done
  68.3 0.0 copy-start.1
  68.3 0.7 copy.23
  68.9 0.1 copy-done.1
  69.0 0.0 copy-start.2
  69.0 0.6 copy.24
  69.6 0.1 copy-done.2
  69.7 0.6 copy.25
Async XLA Ops:
  66.6 1.7 %copy-start = (bf16[2,32768]{1,0:T(2,128)(2,1)S(1)}, bf16[2,32768]{1,0:T(2,128)(2,1)}, u32[]{:S(2)}) copy-start(bf16[2,32768]{1,0:T(2,128)(2,1)} %get-tuple-element.9) | copy-start | bytes 393220
  68.3 0.7 %copy-start.1 = (bf16[2,4096]{1,0:T(2,128)(2,1)S(1)}, bf16[2,4096]{1,0:T(2,128)(2,1)}, u32[]{:S(2)}) copy-start(bf16[2,4096]{1,0:T(2,128)(2,1)} %get-tuple-element.10) | copy-start | bytes 49156
  69.0 0.7 copy-start.2

commit v3 on v2

--- a/solution.py
+++ b/solution.py
@@ -80,6 +80,8 @@
     total,
     top,
     weight_sum,
+    flat_lat,
+    flat_rope,
     in_sem,
     ra_send,
     ra_recv,
@@ -610,7 +612,7 @@
     yd_arrival().wait_recv()
     tile = lat // TILES
     per_block = BLOCK // (2 * PIECE)
-    stored, ropes, flat_scales = [], [], []
+    flat_scales = []
     scale_row = lax.broadcasted_iota(jnp.int32, (BLOCK, BLOCK * TILES), 0)
     scale_lane = lax.broadcasted_iota(jnp.int32, (BLOCK, BLOCK * TILES), 1)
     rope_lane = lax.broadcasted_iota(jnp.int32, (BLOCK, 2 * rope), 1)
@@ -629,26 +631,27 @@
             axis=0,
         ).astype(jnp.float32)
         flat = jnp.zeros((BLOCK, BLOCK * TILES), jnp.float32)
-        tiles = []
+        held = pl.ds(slot * BLOCK, BLOCK)
         for i in range(TILES):
             entries = rows[:, i * tile : (i + 1) * tile]
             scale = jnp.max(jnp.abs(entries), axis=1, keepdims=True) + SCALE_EPS
             scale = scale.astype(jnp.bfloat16).astype(jnp.float32)
-            tiles.append(entries / scale)
+            flat_lat[i, held, :] = entries / scale
             flat = jnp.where(scale_lane == scale_row * TILES + i, scale, flat)
-        stored.append(jnp.concatenate(tiles, axis=1))
         flat_scales.append(jnp.sum(flat, axis=0, keepdims=True))
         tail = rows[:, lat : lat + 2 * rope]
         following = pltpu.roll(pltpu.roll(tail, BLOCK - 1, 0), rope, 1)
-        ropes.append(jnp.where(rope_lane < rope, tail, following))
+        flat_rope[held, :] = jnp.where(rope_lane < rope, tail, following)
     for j in range(BLOCK):
-        cache_lat_ref[:, j * lat : (j + 1) * lat] = jnp.concatenate(
-            [stored[0][j : j + 1], stored[1][j : j + 1]], axis=0
-        ).astype(jnp.bfloat16)
+        for i in range(TILES):
+            first = j * lat + i * tile
+            cache_lat_ref[:, first : first + tile] = flat_lat[
+                i, pl.ds(j, 2, stride=BLOCK), :
+            ].astype(jnp.bfloat16)
     for j in range(BLOCK // 2):
-        cache_rope_ref[:, j * 2 * rope : (j + 1) * 2 * rope] = jnp.concatenate(
-            [ropes[0][2 * j : 2 * j + 1], ropes[1][2 * j : 2 * j + 1]], axis=0
-        ).astype(jnp.bfloat16)
+        cache_rope_ref[:, j * 2 * rope : (j + 1) * 2 * rope] = flat_rope[
+            pl.ds(2 * j, 2, stride=BLOCK), :
+        ].astype(jnp.bfloat16)
     cache_scale_ref[...] = jnp.concatenate(flat_scales, axis=0).astype(jnp.bfloat16)
 
     ra_copy().wait_send()
@@ -739,6 +742,8 @@
             pltpu.VMEM((heads * tok, lat), f32),
             pltpu.VMEM((heads * tok, 128), f32),
             pltpu.VMEM((heads * tok, 128), f32),
+            pltpu.VMEM((TILES, 2 * BLOCK, lat // TILES), f32),
+            pltpu.VMEM((2 * BLOCK, 2 * rope), f32),
             dma((9,)),
             dma,
             dma,

time: 70.5 us -> 70.6 us (level)
  the two profiles are of different devices: /device:TPU:16 before, /device:TPU:8 now
where the time goes in v3:
time: 70.6 us; the launch traced here: 70.3 us
  Pallas kernels  65.4 us (93%)
  local copies, waits for them, and re-layouts  3.67 us (5%)
  between operations  1.3 us (2%)
    pallas_call x1, Pallas kernels, per_device(): pl.pallas_call(functools.partial(kernel, shape), out_shape=(jax.ShapeDtyp...  65.4 us
    unnamed x10, local copies, waits for them, and re-layouts  3.67 us

profile of v3, /device:TPU:8, one launch (start us, length us, event | category | flops | bytes accessed | tf_op | source)
XLA Modules:
  0.0 70.3 jit_solution(1073079229770643801)
XLA Ops:
  1.3 65.4 %shard_map.156 = (bf16[128,1024]{1,0:T(8,128)(2,1)}, bf16[2,32768]{1,0:T(2,128)(2,1)}, bf16[2,4096]{1,0:T(2,128)(2,1)}, bf16[2,256]{1,0:T(2,128)(2,1)}) custom-call(s32[1]{0:T(128)S(6)} %copy.21.length_ref, s32[1,8]{1,0:T(1,128)} %places_ref.1, f32[1,128]{1,0:T(1,128)} %constant.2.clone.frequency_ref, f32[1,512]{1,0:T(1,128)} %bitcast.20, ...), custom_call_target="tpu_custom_call" | custom-call | tf_op jit(solution)/shard_map/pallas_call | solution.py:714
  66.7 0.0 copy-start
  66.7 1.7 %copy.22 = bf16[1,128,1024]{2,1,0:T(8,128)(2,1)} copy(bf16[1,128,1024]{2,1,0:T(8,128)(2,1)} %bitcast.12) | data formatting | bytes 524288
  68.4 0.0 copy-done
  68.4 0.0 copy-start.1
  68.4 0.7 copy.23
  69.0 0.1 copy-done.1
  69.1 0.0 copy-start.2
  69.1 0.6 copy.24
  69.7 0.1 copy-done.2
  69.8 0.6 copy.25
Async XLA Ops:
  66.7 1.7 %copy-start = (bf16[2,32768]{1,0:T(2,128)(2,1)S(1)}, bf16[2,32768]{1,0:T(2,128)(2,1)}, u32[]{:S(2)}) copy-start(bf16[2,32768]{1,0:T(2,128)(2,1)} %get-tuple-element.9) | copy-start | bytes 393220
  68.4 0.7 %copy-start.1 = (bf16[2,4096]{1,0:T(2,128)(2,1)S(1)}, bf16[2,4096]{1,0:T(2,128)(2,1)}, u32[]{:S(2)}) copy-start(bf16[2,4096]{1,0:T(2,128)(2,1)} %get-tuple-element.10) | copy-start | bytes 49156
  69.1 0.7 copy-start.2

commit v4 on v3

v4 whole, which is shorter than its diff:
```python
import functools
import math

import jax
import jax.numpy as jnp
import numpy as np
from jax import lax
from jax.experimental import pallas as pl
from jax.experimental.pallas import tpu as pltpu
from jax.sharding import PartitionSpec as P

MESH = pl.DeviceIdType.MESH
BLOCK = 64
TILES = 4
PIECE = 16
ROWS = 256
ROPE_THETA = 50000.0
NORM_EPS = 1e-06
SCALE_EPS = 1e-06
MASKED = -1e30
FLOOR = -1e28


def when(condition, action):
    if isinstance(condition, bool):
        if condition:
            action()
    else:
        pl.when(condition)(action)


def both(first, second):
    if isinstance(first, bool):
        return first and second
    return jnp.logical_and(first, second)


def sine_cosine(angle):
    turns = jnp.floor(angle * np.float32(1.0 / (2.0 * math.pi)) + 0.5)
    high = 6.28125
    middle = float(np.float32(0.0019350051879882812))
    low = 2.0 * math.pi - high - middle
    r = angle - turns * np.float32(high)
    r = r - turns * np.float32(middle)
    r = r - turns * np.float32(low)
    square = r * r
    sine = jnp.full_like(r, 1.0 / math.factorial(17))
    for n in (15, 13, 11, 9, 7, 5, 3, 1):
        sign = -1.0 if (n // 2) % 2 else 1.0
        sine = sine * square + sign / math.factorial(n)
    cosine = jnp.full_like(r, 1.0 / math.factorial(16))
    for n in (14, 12, 10, 8, 6, 4, 2, 0):
        sign = -1.0 if (n // 2) % 2 else 1.0
        cosine = cosine * square + sign / math.factorial(n)
    return sine * r, cosine


def kernel(
    shape,
    length_ref,
    places_ref,
    frequency_ref,
    gain_ref,
    hidden_hbm,
    q_nope_hbm,
    q_rope_hbm,
    w_latent_hbm,
    w_krope_hbm,
    w_uk_hbm,
    w_uv_hbm,
    pre_lat_hbm,
    pre_rope_hbm,
    out_ref,
    cache_lat_ref,
    cache_rope_ref,
    cache_scale_ref,
    hidden,
    q_nope,
    q_rope,
    w_latent,
    w_krope,
    w_uk,
    w_uv,
    pre_lat,
    pre_rope,
    partial,
    partner_part,
    chip_sum,
    group_part,
    fresh,
    prefix,
    marks,
    blocks,
    queries,
    total,
    top,
    weight_sum,
    flat_rope,
    in_sem,
    ra_send,
    ra_recv,
    rb_send,
    rb_recv,
    own_send,
    own_recv,
    twin_send,
    twin_recv,
    z_send,
    z_recv,
    x_send,
    x_recv,
    d_send,
    d_recv,
    y_send,
    y_recv,
    yd_send,
    yd_recv,
):
    n_rep, n_x, n_hi, n_lo = shape
    n_z = n_hi * n_lo
    half = n_z // 2
    heads, nope, lat = w_uk.shape
    rope = pre_rope.shape[1]
    width = prefix.shape[-1]
    value = w_uv.shape[2]
    tok = hidden.shape[0]

    replica = lax.axis_index("replica")
    context = lax.axis_index("context")
    tensor = lax.axis_index("tensor")
    x = lax.div(context, n_hi)
    z_hi = lax.rem(context, n_hi)
    z_lo = lax.div(tensor, 2)
    core = lax.rem(tensor, 2)
    other = 1 - core
    z = z_hi * n_lo + z_lo
    sign = 1 - 2 * core

    def z_place(step):
        return lax.rem(z + step + n_z, n_z)

    def z_plus(step):
        place = z_place(step)
        return {
            "context": x * n_hi + lax.div(place, n_lo),
            "tensor": lax.rem(place, n_lo) * 2 + core,
        }

    def x_place(step):
        return lax.rem(x + step + n_x, n_x)

    def x_plus(step, who=core):
        return {"context": x_place(step) * n_hi + z_hi, "tensor": z_lo * 2 + who}

    def r_plus(step):
        return lax.rem(replica + step, n_rep)

    def group(step):
        return lax.rem(z_lo + step + n_lo, n_lo)

    partner = {"tensor": z_lo * 2 + other}

    peers = [partner, z_plus(1), z_plus(-1)]
    peers += [x_plus(d, who) for d in range(1, n_x) for who in (core, other)]
    peers += [{"tensor": group(d) * 2 + core} for d in range(1, n_lo)]
    peers += [{"replica": r_plus(d)} for d in range(1, n_rep)]
    barrier = pltpu.get_barrier_semaphore()
    for peer in peers:
        pl.semaphore_signal(barrier, inc=1, device_id=peer, device_id_type=MESH)

    own_pre = pl.multiple_of(z_lo * PIECE, PIECE)
    depth = hidden.shape[1]
    cuts = range(0, depth, 128)
    loads = {
        "prefix": [
            (pre_lat_hbm.at[pl.ds(own_pre, PIECE)], pre_lat),
            (pre_rope_hbm.at[pl.ds(own_pre, PIECE)], pre_rope),
        ],
        "hidden": [(hidden_hbm, hidden), (w_krope_hbm, w_krope)]
        + [
            (w_latent_hbm.at[pl.ds(first, 128)], w_latent.at[pl.ds(first, 128)])
            for first in cuts
        ],
        "query": [(q_nope_hbm, q_nope), (q_rope_hbm, q_rope)]
        + [(w_uk_hbm.at[head], w_uk.at[head]) for head in range(heads)],
        "value": [(w_uv_hbm.at[head], w_uv.at[head]) for head in range(heads)],
    }
    number = 0
    for name, pairs in loads.items():
        copies = []
        for source, target in pairs:
            copies.append(pltpu.make_async_copy(source, target, in_sem.at[number]))
            number += 1
        loads[name] = copies
    for name in ("hidden", "prefix", "query", "value"):
        for load in loads[name]:
            load.start()

    def loaded(name):
        for load in loads[name]:
            load.wait()

    def send(source, target, send_sem, recv_sem, device):
        return pltpu.make_async_remote_copy(
            src_ref=source,
            dst_ref=target,
            send_sem=send_sem,
            recv_sem=recv_sem,
            device_id=device,
            device_id_type=MESH,
        )

    def same(ref, send_sem, recv_sem, device):
        return send(ref, ref, send_sem, recv_sem, device)

    def ra_copy():
        return send(partial.at[other], partner_part, ra_send, ra_recv, partner)

    def rb_copy(d):
        to = lax.rem(z_lo + d, n_lo)
        return send(
            chip_sum.at[to],
            group_part.at[d - 1],
            rb_send.at[d - 1],
            rb_recv.at[d - 1],
            {"tensor": to * 2 + core},
        )

    def slots_of(flow):
        return fresh if flow else prefix

    def own_copies(flow):
        copies = []
        piece = fresh.at[z, x, core] if flow else prefix.at[z, x]
        for d in range(1, n_x):
            for i, who in enumerate((core, other) if flow else (core,)):
                copies.append(
                    same(
                        piece,
                        own_send.at[flow, d - 1, i],
                        own_recv.at[flow, d - 1, core],
                        x_plus(d, who),
                    )
                )
        return copies

    def own_arrival(flow, d, who):
        place = x_place(-d)
        piece = fresh.at[z, place, who] if flow else prefix.at[z, place]
        return same(piece, own_send.at[flow, d - 1, 0], own_recv.at[flow, d - 1, who], partner)

    def own_arrived(flow, d):
        own_arrival(flow, d, core).wait_recv()
        if flow:
            own_arrival(flow, d, other).wait_recv()

    def twin_copy():
        return same(fresh.at[z, x, core], twin_send, twin_recv, partner)

    def twin_arrival():
        return same(fresh.at[z, x, other], twin_send, twin_recv, partner)

    def z_copy(flow, s, i):
        return same(
            slots_of(flow).at[z_place(-sign * (s - 1)), x_place(2 * i)],
            z_send.at[flow, s, i],
            z_recv.at[flow, s, i],
            z_plus(sign),
        )

    def z_arrival(flow, s, i):
        return same(
            slots_of(flow).at[z_place(-sign * s), x_place(2 * i)],
            z_send.at[flow, s, i],
            z_recv.at[flow, s, i],
            partner,
        )

    def x_copy(flow, s, i):
        return same(
            slots_of(flow).at[z_place(-sign * s), x],
            x_send.at[flow, s, i],
            x_recv.at[flow, s, i],
            x_plus(1 - 2 * i),
        )

    def x_arrival(flow, s, i):
        return same(
            slots_of(flow).at[z_place(-sign * s), x_place(2 * i - 1)],
            x_send.at[flow, s, i],
            x_recv.at[flow, s, i],
            partner,
        )

    def d_copy(flow, s):
        return same(
            slots_of(flow).at[z_place(-sign * s)], d_send.at[flow, s], d_recv.at[flow, s], partner
        )

    def d_arrival(flow, s):
        return same(
            slots_of(flow).at[z_place(sign * s)], d_send.at[flow, s], d_recv.at[flow, s], partner
        )

    def come(flow, s):
        z_arrival(flow, s, 0).wait_recv()
        when(s < half, lambda: z_copy(flow, s + 1, 0).start())
        for i in range(2):
            x_copy(flow, s, i).start()
        z_arrival(flow, s, 1).wait_recv()
        when(s < half, lambda: z_copy(flow, s + 1, 1).start())

    def cross(flow, s):
        for i in range(2):
            x_arrival(flow, s, i).wait_recv()
        when(s < half, lambda: d_copy(flow, s).start())

    def stage(flow, s):
        when(s <= half, lambda: come(flow, s))
        when(both(s >= 2, s <= half + 1), lambda: cross(flow, s - 1))
        when(both(s >= 3, s <= half + 1), lambda: d_arrival(flow, s - 2).wait_recv())

    def y_copy(d):
        return send(
            fresh.at[pl.ds(z_hi * n_lo, n_lo), x, core],
            blocks.at[core, pl.ds(replica * n_lo, n_lo)],
            y_send.at[d - 1],
            y_recv.at[d - 1],
            {"replica": r_plus(d)},
        )

    def y_arrival(d):
        return send(
            fresh.at[pl.ds(z_hi * n_lo, n_lo), x, core],
            blocks.at[core, pl.ds(r_plus(n_rep - d) * n_lo, n_lo)],
            y_send.at[d - 1],
            y_recv.at[d - 1],
            partner,
        )

    def yd_copy():
        return same(blocks.at[core], yd_send, yd_recv, partner)

    def yd_arrival():
        return same(blocks.at[other], yd_send, yd_recv, partner)

    loaded("hidden")
    lat_term = jnp.dot(hidden[...], w_latent[...], preferred_element_type=jnp.float32)
    rope_term = lax.dot_general(
        hidden[...], w_krope[...], (((1,), (1,)), ((), ())), preferred_element_type=jnp.float32
    )
    rope_term = jnp.concatenate(
        [rope_term, jnp.zeros((tok, width - lat - rope), jnp.float32)], axis=1
    )
    for place in range(n_lo):
        for who in range(2):
            first = (place * 2 + who) * PIECE
            partial[who, place, :, :lat] = lat_term[first : first + PIECE]
            partial[who, place, :, lat:] = rope_term[first : first + PIECE]
    loaded("prefix")
    prefix[z, x, :, :lat] = pre_lat[...]
    length = length_ref[0]
    n_context = n_x * n_hi
    piece_row = lax.broadcasted_iota(jnp.int32, (PIECE, width - lat), 0)
    piece_lanes = lax.broadcasted_iota(jnp.int32, (PIECE, width - lat), 1)
    pre_place = context * (n_lo * PIECE) + z_lo * PIECE + piece_row
    hidden_key = jnp.logical_and(piece_lanes == rope + n_context, pre_place >= length)
    pre_tail = jnp.concatenate(
        [
            pre_rope[...].astype(jnp.float32),
            jnp.zeros((PIECE, width - lat - rope), jnp.float32),
        ],
        axis=1,
    )
    prefix[z, x, :, lat:] = jnp.where(hidden_key, MASKED, pre_tail).astype(
        jnp.bfloat16
    )

    pl.semaphore_wait(barrier, len(peers))
    ra_copy().start()
    z_copy(0, 1, 0).start()
    for copy in own_copies(0):
        copy.start()

    loaded("query")
    lanes = lax.broadcasted_iota(jnp.int32, (tok, width - lat), 1)
    later = jnp.logical_and(lanes > rope + context, lanes < rope + n_context)
    masks = jnp.where(later, MASKED, jnp.where(lanes == rope + n_context, 1.0, 0.0))
    query_row = lax.broadcasted_iota(jnp.int32, (tok, tok), 0)
    key_lane = lax.broadcasted_iota(jnp.int32, (tok, tok), 1)
    triangle = jnp.where(key_lane > query_row, MASKED, 0.0).astype(jnp.bfloat16)
    marks[...] = jnp.zeros_like(marks)
    mark_row = lax.broadcasted_iota(jnp.int32, (PIECE, tok), 0)
    mark_lane = lax.broadcasted_iota(jnp.int32, (PIECE, tok), 1)
    for place in range(n_lo):
        for who in range(2):
            first = (place * 2 + who) * PIECE
            marks[z_hi * n_lo + place, x, who] = jnp.where(
                mark_lane == first + mark_row, 1.0, 0.0
            ).astype(jnp.bfloat16)

    def absorb(first, last):
        for head in range(first, last):
            rows = pl.ds(head * tok, tok)
            queries[rows, :lat] = jnp.dot(
                q_nope[:, head * nope : (head + 1) * nope],
                w_uk[head],
                preferred_element_type=jnp.float32,
            ).astype(jnp.bfloat16)
            pair = q_rope[:, (head // 2) * 2 * rope : (head // 2 + 1) * 2 * rope]
            pair = pair.astype(jnp.float32)
            if head % 2:
                pair = pltpu.roll(pair, rope, 1)
            queries[rows, lat:width] = jnp.where(lanes < rope, pair, masks).astype(jnp.bfloat16)
            queries[rows, width:] = triangle

    absorb(0, heads // 2)

    ra_copy().wait_recv()
    chip_sum[...] = partial[core] + partner_part[...]
    for d in range(1, n_lo):
        rb_copy(d).start()

    own_arrived(0, 2)
    z_copy(0, 1, 1).start()
    absorb(heads // 2, heads)

    position = (
        length
        + context * tok
        + tensor * PIECE
        + piece_row
    )
    sine, cosine = sine_cosine(position.astype(jnp.float32) * frequency_ref[...])
    sine = jnp.where(piece_lanes < rope // 2, -sine, sine)
    sine = jnp.where(piece_lanes < rope, sine, 0.0)

    top[...] = jnp.full_like(top, FLOOR)
    weight_sum[...] = jnp.zeros_like(weight_sum)
    total[...] = jnp.zeros_like(total)

    stage(0, 1)
    for d in range(1, n_lo):
        rb_copy(d).wait_recv()
    summed = chip_sum[z_lo]
    for d in range(1, n_lo):
        summed = summed + group_part[d - 1]
    lat_sum = summed[:, :lat]
    mean_square = jnp.mean(lat_sum * lat_sum, axis=1, keepdims=True)
    fresh[z, x, core, :, :lat] = (
        lat_sum * lax.rsqrt(mean_square + NORM_EPS) * gain_ref[...]
    ).astype(jnp.bfloat16)
    rope_sum = summed[:, lat:]
    swapped = jnp.where(
        piece_lanes < rope // 2,
        pltpu.roll(rope_sum, width - lat - rope // 2, 1),
        pltpu.roll(rope_sum, rope // 2, 1),
    )
    new_tail = rope_sum * cosine + swapped * sine
    fresh[z, x, core, :, lat:] = jnp.where(
        piece_lanes == rope + context, 1.0, new_tail
    ).astype(jnp.bfloat16)

    twin_copy().start()
    for copy in own_copies(1):
        copy.start()
    stage(0, 2)
    twin_arrival().wait_recv()
    z_copy(1, 1, 0).start()
    own_arrived(1, 2)
    z_copy(1, 1, 1).start()
    for d in (1, 3):
        own_arrived(0, d)
    stage(0, 3)

    score_scale = float((nope + rope) ** (-0.5) * math.log2(math.e))

    zeros = jnp.zeros((n_x * PIECE, tok), jnp.bfloat16)

    def attend(slots):
        count = n_x * PIECE
        parts = []
        for place in slots:
            parts.append((fresh[place].reshape(2 * count, width), marks[place].reshape(2 * count, tok)))
            parts.append((prefix[place].reshape(count, width), zeros))
        key_rows = jnp.concatenate(
            [jnp.concatenate(part, axis=1) for part in parts], axis=0
        )
        tiles = len(slots) * 3 * count // 128
        at_once = min(ROWS, heads * tok)
        for first in range(0, heads * tok, at_once):
            rows = pl.ds(first, at_once)
            scores = lax.dot_general(
                queries[rows, :],
                key_rows,
                (((1,), (1,)), ((), ())),
                preferred_element_type=jnp.float32,
            )
            scores = scores * score_scale
            old_top = top[rows, :]
            new_top = jnp.maximum(old_top, jnp.max(scores, axis=1, keepdims=True))
            top[rows, :] = new_top
            rescale = jnp.exp2(old_top - new_top)
            exponents = [
                jnp.exp2(scores[:, i * 128 : (i + 1) * 128] - new_top) for i in range(tiles)
            ]
            weight_sum[rows, :] = weight_sum[rows, :] * rescale + sum(exponents)
            weights = jnp.concatenate([e.astype(jnp.bfloat16) for e in exponents], axis=1)
            total[rows, :] = total[rows, :] * jnp.concatenate(
                [rescale] * (lat // 128), axis=1
            ) + jnp.dot(weights, key_rows[:, :lat], preferred_element_type=jnp.float32)


    def to_owners():
        for d in range(1, n_rep):
            y_copy(d).start()
        for place in range(n_lo):
            blocks[core, replica * n_lo + place] = fresh[z_hi * n_lo + place, x, core]

    def owners():
        for d in range(1, n_rep):
            y_arrival(d).wait_recv()
        yd_copy().start()

    def own_slot():
        for d in (1, 3):
            own_arrived(1, d)

    def iteration(s, carry):
        stage(1, s)
        stage(0, s + 3)
        pl.when(s == 2)(own_slot)
        pl.when(s == n_lo + 1)(to_owners)
        pl.when(s == half + 1)(owners)
        pl.when(s >= 3)(
            lambda: attend(
                [z_place(s - 2), jnp.where(s == half + 2, z, z_place(2 - s))]
            )
        )
        return carry

    lax.fori_loop(1, half + 3, iteration, 0)

    loaded("value")
    for head in range(heads):
        rows = pl.ds(head * tok, tok)
        row_sum = jnp.sum(weight_sum[rows, :], axis=1, keepdims=True)
        latent_out = (total[rows, :] / row_sum).astype(jnp.bfloat16)
        out_ref[:, head * value : (head + 1) * value] = jnp.dot(
            latent_out, w_uv[head], preferred_element_type=jnp.float32
        ).astype(jnp.bfloat16)

    yd_arrival().wait_recv()
    tile = lat // TILES
    per_block = BLOCK // (2 * PIECE)
    flat_scales = []
    scale_row = lax.broadcasted_iota(jnp.int32, (BLOCK, BLOCK * TILES), 0)
    scale_lane = lax.broadcasted_iota(jnp.int32, (BLOCK, BLOCK * TILES), 1)
    rope_lane = lax.broadcasted_iota(jnp.int32, (BLOCK, 2 * rope), 1)
    for slot in range(2):
        source = jnp.int32(0)
        for candidate in range(n_rep * 2):
            source = jnp.where(
                places_ref[0, candidate] == replica * 2 + slot, candidate, source
            )
        rows = jnp.concatenate(
            [
                blocks[who, source * per_block + place]
                for place in range(per_block)
                for who in range(2)
            ],
            axis=0,
        ).astype(jnp.float32)
        flat = jnp.zeros((BLOCK, BLOCK * TILES), jnp.float32)
        held = pl.ds(slot * BLOCK, BLOCK)
        for i in range(TILES):
            entries = rows[:, i * tile : (i + 1) * tile]
            scale = jnp.max(jnp.abs(entries), axis=1, keepdims=True) + SCALE_EPS
            scale = scale.astype(jnp.bfloat16).astype(jnp.float32)
            cache_lat_ref[slot, :, i * tile : (i + 1) * tile] = (entries / scale).astype(
                jnp.bfloat16
            )
            flat = jnp.where(scale_lane == scale_row * TILES + i, scale, flat)
        flat_scales.append(jnp.sum(flat, axis=0, keepdims=True))
        tail = rows[:, lat : lat + 2 * rope]
        following = pltpu.roll(pltpu.roll(tail, BLOCK - 1, 0), rope, 1)
        flat_rope[held, :] = jnp.where(rope_lane < rope, tail, following)
    for j in range(BLOCK // 2):
        cache_rope_ref[:, j * 2 * rope : (j + 1) * 2 * rope] = flat_rope[
            pl.ds(2 * j, 2, stride=BLOCK), :
        ].astype(jnp.bfloat16)
    cache_scale_ref[...] = jnp.concatenate(flat_scales, axis=0).astype(jnp.bfloat16)

    ra_copy().wait_send()
    for d in range(1, n_lo):
        rb_copy(d).wait_send()
    for d in range(1, n_rep):
        y_copy(d).wait_send()
    yd_copy().wait_send()

    twin_copy().wait_send()
    for flow in range(2):
        for copy in own_copies(flow):
            copy.wait_send()

    def sent(s, carry):
        for flow in range(2):
            for i in range(2):
                z_copy(flow, s, i).wait_send()
                x_copy(flow, s, i).wait_send()
            pl.when(s < half)(lambda: d_copy(flow, s).wait_send())
        return carry

    lax.fori_loop(1, half + 1, sent, 0)


def per_device(
    shape,
    hidden,
    q_nope,
    q_rope,
    w_latent,
    w_krope,
    kv_gain,
    w_uk,
    w_uv,
    prefix_latent,
    prefix_rope,
    prefix_lengths,
    placements,
):
    n_rep, n_x, n_hi, n_lo = shape
    n_z = n_hi * n_lo
    half = n_z // 2
    tok, depth = hidden.shape[1:]
    heads, nope, lat = w_uk.shape
    rope = w_krope.shape[1]
    value = w_uv.shape[2]
    width = -(-(lat + rope) // 128) * 128
    count = rope // 2
    powers = -(np.arange(count, dtype=np.float32) * np.float32(2.0)) / np.float32(rope)
    frequency = np.power(np.float64(ROPE_THETA), powers.astype(np.float64))
    frequency = np.resize(frequency, (1, width - lat)).astype(np.float32)
    vmem = pl.BlockSpec(memory_space=pltpu.VMEM)
    smem = pl.BlockSpec(memory_space=pltpu.SMEM)
    anywhere = pl.BlockSpec(memory_space=pl.ANY)
    bf16, f32 = jnp.bfloat16, jnp.float32
    dma = pltpu.SemaphoreType.DMA
    out = pl.pallas_call(
        functools.partial(kernel, shape),
        out_shape=(
            jax.ShapeDtypeStruct((tok, heads * value), bf16),
            jax.ShapeDtypeStruct((2, BLOCK, lat), bf16),
            jax.ShapeDtypeStruct((2, BLOCK * rope), bf16),
            jax.ShapeDtypeStruct((2, BLOCK * TILES), bf16),
        ),
        in_specs=[smem, smem, vmem, vmem] + [anywhere] * 9,
        out_specs=(vmem, vmem, vmem, vmem),
        scratch_shapes=[
            pltpu.VMEM((tok, depth), bf16),
            pltpu.VMEM((tok, heads * nope), bf16),
            pltpu.VMEM((tok, heads * rope), bf16),
            pltpu.VMEM((depth, lat), bf16),
            pltpu.VMEM((rope, depth), bf16),
            pltpu.VMEM((heads, nope, lat), bf16),
            pltpu.VMEM((heads, lat, value), bf16),
            pltpu.VMEM((PIECE, lat), bf16),
            pltpu.VMEM((PIECE, rope), bf16),
            pltpu.VMEM((2, n_lo, PIECE, width), f32),
            pltpu.VMEM((n_lo, PIECE, width), f32),
            pltpu.VMEM((n_lo, PIECE, width), f32),
            pltpu.VMEM((max(n_lo - 1, 1), PIECE, width), f32),
            pltpu.VMEM((n_z, n_x, 2, PIECE, width), bf16),
            pltpu.VMEM((n_z, n_x, PIECE, width), bf16),
            pltpu.VMEM((n_z, n_x, 2, PIECE, tok), bf16),
            pltpu.VMEM((2, n_rep * n_lo, PIECE, width), bf16),
            pltpu.VMEM((heads * tok, width + tok), bf16),
            pltpu.VMEM((heads * tok, lat), f32),
            pltpu.VMEM((heads * tok, 128), f32),
            pltpu.VMEM((heads * tok, 128), f32),
            pltpu.VMEM((2 * BLOCK, 2 * rope), f32),
            dma((6 + depth // 128 + 2 * heads,)),
            dma,
            dma,
            dma((max(n_lo - 1, 1),)),
            dma((max(n_lo - 1, 1),)),
            dma((2, n_x - 1, 2)),
            dma((2, n_x - 1, 2)),
            dma,
            dma,
            dma((2, half + 1, 2)),
            dma((2, half + 1, 2)),
            dma((2, half + 1, 2)),
            dma((2, half + 1, 2)),
            dma((2, half + 1)),
            dma((2, half + 1)),
            dma((max(n_rep - 1, 1),)),
            dma((max(n_rep - 1, 1),)),
            dma,
            dma,
        ],
        compiler_params=pltpu.CompilerParams(
            collective_id=0, has_side_effects=True, vmem_limit_bytes=56 * 1024 * 1024
        ),
    )(
        prefix_lengths,
        placements,
        jnp.asarray(frequency),
        kv_gain.reshape(1, lat),
        hidden[0],
        q_nope[0],
        q_rope[0],
        w_latent,
        w_krope.T,
        w_uk,
        w_uv,
        prefix_latent[0],
        prefix_rope[0],
    )
    return tuple(result.reshape(1, result.shape[0], -1) for result in out)


def program(mesh, shape):
    return jax.shard_map(
        functools.partial(per_device, shape),
        mesh=mesh,
        in_specs=(
            P("replica", "context", "tensor"),
            P("replica", "context", "tensor"),
            P("replica", "context", "tensor"),
            P("tensor", None),
            P("tensor", None),
            P(),
            P("tensor", None, None),
            P("tensor", None, None),
            P("replica", "context", None),
            P("replica", "context", None),
            P("replica"),
            P("context", None),
        ),
        out_specs=(
            P("replica", "context", "tensor"),
            P("replica", "context", None),
            P("replica", "context", None),
            P("replica", "context", None),
        ),
        check_vma=False,
    )


def solution(mesh):
    n_hi = 4
    return program(
        mesh,
        (
            mesh.shape["replica"],
            mesh.shape["context"] // n_hi,
            n_hi,
            mesh.shape["tensor"] // 2,
        ),
    )
```

time: 70.6 us -> 68.3 us (0.967)
  the two profiles are of different devices: /device:TPU:8 before, /device:TPU:1 now
where the time goes in v4:
time: 68.3 us; the launch traced here: 68.1 us
  Pallas kernels  63.2 us (93%)
  local copies, waits for them, and re-layouts  3.64 us (5%)
  between operations  1.3 us (2%)
    pallas_call x1, Pallas kernels, per_device(): pl.pallas_call(functools.partial(kernel, shape), out_shape=(jax.ShapeDtyp...  63.2 us
    unnamed x9, local copies, waits for them, and re-layouts  1.96 us
    reshape x1, local copies, waits for them, and re-layouts, per_device(): return tuple((result.reshape(1, result.shape[0], -1) for result in out))  1.68 us

profile of v4, /device:TPU:1, one launch (start us, length us, event | category | flops | bytes accessed | tf_op | source)
XLA Modules:
  0.0 68.1 jit_solution(8177518378565791404)
XLA Ops:
  1.3 63.2 %shard_map.156 = (bf16[128,1024]{1,0:T(8,128)(2,1)}, bf16[2,64,512]{2,1,0:T(8,128)(2,1)}, bf16[2,4096]{1,0:T(2,128)(2,1)}, bf16[2,256]{1,0:T(2,128)(2,1)}) custom-call(s32[1]{0:T(128)S(6)} %copy.20.length_ref, s32[1,8]{1,0:T(1,128)} %places_ref.1, f32[1,128]{1,0:T(1,128)} %constant.2.clone.frequency_ref, f32[1,512]{1,0:T(1,128)} %bitcast.18, ...), custom_call_target="tpu_custom_call" | custom-call | tf_op jit(solution)/shard_map/pallas_call | solution.py:649
  64.4 0.0 copy-start
  64.5 1.7 %reshape.25 = bf16[1,2,32768]{2,1,0:T(2,128)(2,1)} reshape(bf16[2,64,512]{2,1,0:T(8,128)(2,1)} %get-tuple-element.9) | data formatting | bytes 262144 | tf_op jit(solution)/shard_map/reshape | solution.py:720
  66.1 0.0 copy-done
  66.1 0.0 copy-start.1
  66.1 0.7 %copy.21 = bf16[1,128,1024]{2,1,0:T(8,128)(2,1)} copy(bf16[1,128,1024]{2,1,0:T(8,128)(2,1)S(1)} %bitcast.11) | data formatting | bytes 524288
  66.8 0.0 copy-done.1
  66.9 0.0 copy-start.2
  66.9 0.6 copy.22
  67.5 0.1 copy-done.2
  67.5 0.6 copy.23
Async XLA Ops:
  64.4 1.7 %copy-start = (bf16[128,1024]{1,0:T(8,128)(2,1)S(1)}, bf16[128,1024]{1,0:T(8,128)(2,1)}, u32[]{:S(2)}) copy-start(bf16[128,1024]{1,0:T(8,128)(2,1)} %get-tuple-element.8) | copy-start | bytes 786436
  66.1 0.7 %copy-start.1 = (bf16[2,4096]{1,0:T(2,128)(2,1)S(1)}, bf16[2,4096]{1,0:T(2,128)(2,1)}, u32[]{:S(2)}) copy-start(bf16[2,4096]{1,0:T(2,128)(2,1)} %get-tuple-element.10) | copy-start | bytes 49156
  66.9 0.7 copy-start.2

commit v5 on v4

--- a/solution.py
+++ b/solution.py
@@ -13,7 +13,7 @@
 BLOCK = 64
 TILES = 4
 PIECE = 16
-ROWS = 256
+ROWS = 512
 ROPE_THETA = 50000.0
 NORM_EPS = 1e-06
 SCALE_EPS = 1e-06
@@ -475,23 +475,23 @@
 
     score_scale = float((nope + rope) ** (-0.5) * math.log2(math.e))
 
-    zeros = jnp.zeros((n_x * PIECE, tok), jnp.bfloat16)
-
-    def attend(slots):
-        count = n_x * PIECE
-        parts = []
-        for place in slots:
-            parts.append((fresh[place].reshape(2 * count, width), marks[place].reshape(2 * count, tok)))
-            parts.append((prefix[place].reshape(count, width), zeros))
-        key_rows = jnp.concatenate(
-            [jnp.concatenate(part, axis=1) for part in parts], axis=0
-        )
-        tiles = len(slots) * 3 * count // 128
+    def new_keys(place):
+        count = 2 * n_x * PIECE
+        return jnp.concatenate(
+            [fresh[place].reshape(count, width), marks[place].reshape(count, tok)], axis=1
+        )
+
+    def prefix_keys(place):
+        return prefix[place].reshape(n_x * PIECE, width)
+
+    def attend(parts):
+        key_rows = jnp.concatenate(parts, axis=0)
+        tiles, depth = key_rows.shape[0] // 128, key_rows.shape[1]
         at_once = min(ROWS, heads * tok)
         for first in range(0, heads * tok, at_once):
             rows = pl.ds(first, at_once)
             scores = lax.dot_general(
-                queries[rows, :],
+                queries[rows, :depth],
                 key_rows,
                 (((1,), (1,)), ((), ())),
                 preferred_element_type=jnp.float32,
@@ -532,9 +532,18 @@
         pl.when(s == 2)(own_slot)
         pl.when(s == n_lo + 1)(to_owners)
         pl.when(s == half + 1)(owners)
+
+        def attend_prefix():
+            last = jnp.where(s + 1 == half, z, z_place(-s - 1))
+            attend([prefix_keys(place) for place in (z_place(s), z_place(-s), z_place(s + 1), last)])
+
+        pl.when(both(lax.rem(s, 2) == 1, s < half))(attend_prefix)
         pl.when(s >= 3)(
             lambda: attend(
-                [z_place(s - 2), jnp.where(s == half + 2, z, z_place(2 - s))]
+                [
+                    new_keys(z_place(s - 2)),
+                    new_keys(jnp.where(s == half + 2, z, z_place(2 - s))),
+                ]
             )
         )
         return carry

time: 68.3 us -> 70 us (1.025)
  Pallas kernels: 63.2 us -> 64.7 us
    pallas_call x1, Pallas kernels: 63.2 us -> 64.7 us  [per_device(): pl.pallas_call(functools.partial(kernel, shape), out_shape=(jax.ShapeDtyp...]
where the time goes in v5:
time: 70 us; the launch traced here: 69.6 us
  Pallas kernels  64.7 us (92%)
  local copies, waits for them, and re-layouts  3.64 us (5%)
  between operations  1.3 us (2%)
    pallas_call x1, Pallas kernels, per_device(): pl.pallas_call(functools.partial(kernel, shape), out_shape=(jax.ShapeDtyp...  64.7 us
    unnamed x9, local copies, waits for them, and re-layouts  1.96 us
    reshape x1, local copies, waits for them, and re-layouts, per_device(): return tuple((result.reshape(1, result.shape[0], -1) for result in out))  1.68 us

profile of v5, /device:TPU:1, one launch (start us, length us, event | category | flops | bytes accessed | tf_op | source)
XLA Modules:
  0.0 69.6 jit_solution(10203271708957787867)
XLA Ops:
  1.3 64.7 %shard_map.156 = (bf16[128,1024]{1,0:T(8,128)(2,1)}, bf16[2,64,512]{2,1,0:T(8,128)(2,1)}, bf16[2,4096]{1,0:T(2,128)(2,1)}, bf16[2,256]{1,0:T(2,128)(2,1)}) custom-call(s32[1]{0:T(128)S(6)} %copy.20.length_ref, s32[1,8]{1,0:T(1,128)} %places_ref.1, f32[1,128]{1,0:T(1,128)} %constant.2.clone.frequency_ref, f32[1,512]{1,0:T(1,128)} %bitcast.18, ...), custom_call_target="tpu_custom_call" | custom-call | tf_op jit(solution)/shard_map/pallas_call | solution.py:658
  66.0 0.0 copy-start
  66.0 1.7 %reshape.25 = bf16[1,2,32768]{2,1,0:T(2,128)(2,1)} reshape(bf16[2,64,512]{2,1,0:T(8,128)(2,1)} %get-tuple-element.9) | data formatting | bytes 262144 | tf_op jit(solution)/shard_map/reshape | solution.py:729
  67.7 0.0 copy-done
  67.7 0.0 copy-start.1
  67.7 0.7 %copy.21 = bf16[1,128,1024]{2,1,0:T(8,128)(2,1)} copy(bf16[1,128,1024]{2,1,0:T(8,128)(2,1)S(1)} %bitcast.11) | data formatting | bytes 524288
  68.4 0.0 copy-done.1
  68.4 0.0 copy-start.2
  68.4 0.6 copy.22
  69.0 0.1 copy-done.2
  69.1 0.6 copy.23
Async XLA Ops:
  66.0 1.7 %copy-start = (bf16[128,1024]{1,0:T(8,128)(2,1)S(1)}, bf16[128,1024]{1,0:T(8,128)(2,1)}, u32[]{:S(2)}) copy-start(bf16[128,1024]{1,0:T(8,128)(2,1)} %get-tuple-element.8) | copy-start | bytes 786436
  67.7 0.7 %copy-start.1 = (bf16[2,4096]{1,0:T(2,128)(2,1)S(1)}, bf16[2,4096]{1,0:T(2,128)(2,1)}, u32[]{:S(2)}) copy-start(bf16[2,4096]{1,0:T(2,128)(2,1)} %get-tuple-element.10) | copy-start | bytes 49156
  68.4 0.7 copy-start.2

commit v6 on v4

--- a/solution.py
+++ b/solution.py
@@ -113,8 +113,6 @@
     d_recv,
     y_send,
     y_recv,
-    yd_send,
-    yd_recv,
 ):
     n_rep, n_x, n_hi, n_lo = shape
     n_z = n_hi * n_lo
@@ -163,7 +161,11 @@
     peers = [partner, z_plus(1), z_plus(-1)]
     peers += [x_plus(d, who) for d in range(1, n_x) for who in (core, other)]
     peers += [{"tensor": group(d) * 2 + core} for d in range(1, n_lo)]
-    peers += [{"replica": r_plus(d)} for d in range(1, n_rep)]
+    peers += [
+        {"replica": r_plus(d), "tensor": z_lo * 2 + who}
+        for d in range(1, n_rep)
+        for who in (core, other)
+    ]
     barrier = pltpu.get_barrier_semaphore()
     for peer in peers:
         pl.semaphore_signal(barrier, inc=1, device_id=peer, device_id_type=MESH)
@@ -276,73 +278,85 @@
             partner,
         )
 
-    def x_copy(flow, s, i):
+    def x_copy(flow, s, i, who):
         return same(
             slots_of(flow).at[z_place(-sign * s), x],
-            x_send.at[flow, s, i],
-            x_recv.at[flow, s, i],
-            x_plus(1 - 2 * i),
-        )
-
-    def x_arrival(flow, s, i):
+            x_send.at[flow, s, i, who],
+            x_recv.at[flow, s, i, core],
+            x_plus(1 - 2 * i, who),
+        )
+
+    def x_arrival(flow, s, i, who):
         return same(
-            slots_of(flow).at[z_place(-sign * s), x_place(2 * i - 1)],
-            x_send.at[flow, s, i],
-            x_recv.at[flow, s, i],
+            slots_of(flow).at[z_place((2 * who - 1) * s), x_place(2 * i - 1)],
+            x_send.at[flow, s, i, who],
+            x_recv.at[flow, s, i, who],
             partner,
         )
 
-    def d_copy(flow, s):
+    def d_copy(flow, s, i):
         return same(
-            slots_of(flow).at[z_place(-sign * s)], d_send.at[flow, s], d_recv.at[flow, s], partner
-        )
-
-    def d_arrival(flow, s):
+            slots_of(flow).at[z_place(-sign * s), x_place(2 * i)],
+            d_send.at[flow, s, i],
+            d_recv.at[flow, s, i],
+            partner,
+        )
+
+    def d_arrival(flow, s, i):
         return same(
-            slots_of(flow).at[z_place(sign * s)], d_send.at[flow, s], d_recv.at[flow, s], partner
+            slots_of(flow).at[z_place(sign * s), x_place(2 * i)],
+            d_send.at[flow, s, i],
+            d_recv.at[flow, s, i],
+            partner,
         )
 
     def come(flow, s):
+        def to_other_cores():
+            for i in range(2):
+                x_copy(flow, s, i, other).start()
+            d_copy(flow, s, 0).start()
+
         z_arrival(flow, s, 0).wait_recv()
         when(s < half, lambda: z_copy(flow, s + 1, 0).start())
         for i in range(2):
-            x_copy(flow, s, i).start()
+            x_copy(flow, s, i, core).start()
+        when(s < half, to_other_cores)
         z_arrival(flow, s, 1).wait_recv()
         when(s < half, lambda: z_copy(flow, s + 1, 1).start())
-
-    def cross(flow, s):
+        when(s < half, lambda: d_copy(flow, s, 1).start())
+
+    def settle(flow, s):
         for i in range(2):
-            x_arrival(flow, s, i).wait_recv()
-        when(s < half, lambda: d_copy(flow, s).start())
+            x_arrival(flow, s, i, core).wait_recv()
+
+        def from_other_cores():
+            for i in range(2):
+                x_arrival(flow, s, i, other).wait_recv()
+                d_arrival(flow, s, i).wait_recv()
+
+        when(s < half, from_other_cores)
 
     def stage(flow, s):
         when(s <= half, lambda: come(flow, s))
-        when(both(s >= 2, s <= half + 1), lambda: cross(flow, s - 1))
-        when(both(s >= 3, s <= half + 1), lambda: d_arrival(flow, s - 2).wait_recv())
-
-    def y_copy(d):
+        when(both(s >= 2, s <= half + 1), lambda: settle(flow, s - 1))
+
+    def y_copy(d, who):
         return send(
             fresh.at[pl.ds(z_hi * n_lo, n_lo), x, core],
             blocks.at[core, pl.ds(replica * n_lo, n_lo)],
-            y_send.at[d - 1],
-            y_recv.at[d - 1],
-            {"replica": r_plus(d)},
-        )
-
-    def y_arrival(d):
+            y_send.at[d - 1, who],
+            y_recv.at[d - 1, core],
+            {"replica": r_plus(d), "tensor": z_lo * 2 + who},
+        )
+
+    def y_arrival(d, who):
         return send(
             fresh.at[pl.ds(z_hi * n_lo, n_lo), x, core],
-            blocks.at[core, pl.ds(r_plus(n_rep - d) * n_lo, n_lo)],
-            y_send.at[d - 1],
-            y_recv.at[d - 1],
+            blocks.at[who, pl.ds(r_plus(n_rep - d) * n_lo, n_lo)],
+            y_send.at[d - 1, who],
+            y_recv.at[d - 1, who],
             partner,
         )
-
-    def yd_copy():
-        return same(blocks.at[core], yd_send, yd_recv, partner)
-
-    def yd_arrival():
-        return same(blocks.at[other], yd_send, yd_recv, partner)
 
     loaded("hidden")
     lat_term = jnp.dot(hidden[...], w_latent[...], preferred_element_type=jnp.float32)
@@ -513,14 +527,11 @@
 
     def to_owners():
         for d in range(1, n_rep):
-            y_copy(d).start()
+            for who in (core, other):
+                y_copy(d, who).start()
         for place in range(n_lo):
-            blocks[core, replica * n_lo + place] = fresh[z_hi * n_lo + place, x, core]
-
-    def owners():
-        for d in range(1, n_rep):
-            y_arrival(d).wait_recv()
-        yd_copy().start()
+            for who in range(2):
+                blocks[who, replica * n_lo + place] = fresh[z_hi * n_lo + place, x, who]
 
     def own_slot():
         for d in (1, 3):
@@ -530,16 +541,15 @@
         stage(1, s)
         stage(0, s + 3)
         pl.when(s == 2)(own_slot)
-        pl.when(s == n_lo + 1)(to_owners)
-        pl.when(s == half + 1)(owners)
-        pl.when(s >= 3)(
+        pl.when(s == n_lo)(to_owners)
+        pl.when(s >= 2)(
             lambda: attend(
-                [z_place(s - 2), jnp.where(s == half + 2, z, z_place(2 - s))]
+                [z_place(s - 1), jnp.where(s == half + 1, z, z_place(1 - s))]
             )
         )
         return carry
 
-    lax.fori_loop(1, half + 3, iteration, 0)
+    lax.fori_loop(1, half + 2, iteration, 0)
 
     loaded("value")
     for head in range(heads):
@@ -550,7 +560,9 @@
             latent_out, w_uv[head], preferred_element_type=jnp.float32
         ).astype(jnp.bfloat16)
 
-    yd_arrival().wait_recv()
+    for d in range(1, n_rep):
+        for who in (core, other):
+            y_arrival(d, who).wait_recv()
     tile = lat // TILES
     per_block = BLOCK // (2 * PIECE)
     flat_scales = []
@@ -595,8 +607,8 @@
     for d in range(1, n_lo):
         rb_copy(d).wait_send()
     for d in range(1, n_rep):
-        y_copy(d).wait_send()
-    yd_copy().wait_send()
+        for who in (core, other):
+            y_copy(d, who).wait_send()
 
     twin_copy().wait_send()
     for flow in range(2):
@@ -607,8 +619,14 @@
         for flow in range(2):
             for i in range(2):
                 z_copy(flow, s, i).wait_send()
-                x_copy(flow, s, i).wait_send()
-            pl.when(s < half)(lambda: d_copy(flow, s).wait_send())
+                x_copy(flow, s, i, core).wait_send()
+
+            def to_other_cores():
+                for i in range(2):
+                    x_copy(flow, s, i, other).wait_send()
+                    d_copy(flow, s, i).wait_send()
+
+            pl.when(s < half)(to_other_cores)
         return carry
 
     lax.fori_loop(1, half + 1, sent, 0)
@@ -690,14 +708,12 @@
             dma,
             dma((2, half + 1, 2)),
             dma((2, half + 1, 2)),
+            dma((2, half + 1, 2, 2)),
+            dma((2, half + 1, 2, 2)),
             dma((2, half + 1, 2)),
             dma((2, half + 1, 2)),
-            dma((2, half + 1)),
-            dma((2, half + 1)),
-            dma((max(n_rep - 1, 1),)),
-            dma((max(n_rep - 1, 1),)),
-            dma,
-            dma,
+            dma((max(n_rep - 1, 1), 2)),
+            dma((max(n_rep - 1, 1), 2)),
         ],
         compiler_params=pltpu.CompilerParams(
             collective_id=0, has_side_effects=True, vmem_limit_bytes=56 * 1024 * 1024

time: 68.3 us -> 69.6 us (1.019)
  Pallas kernels: 63.2 us -> 64.4 us
    pallas_call x1, Pallas kernels: 63.2 us -> 64.4 us  [per_device(): pl.pallas_call(functools.partial(kernel, shape), out_shape=(jax.ShapeDtyp...]
where the time goes in v6:
time: 69.6 us; the launch traced here: 69.3 us
  Pallas kernels  64.4 us (93%)
  local copies, waits for them, and re-layouts  3.64 us (5%)
  between operations  1.3 us (2%)
    pallas_call x1, Pallas kernels, per_device(): pl.pallas_call(functools.partial(kernel, shape), out_shape=(jax.ShapeDtyp...  64.4 us
    unnamed x9, local copies, waits for them, and re-layouts  1.96 us
    reshape x1, local copies, waits for them, and re-layouts, per_device(): return tuple((result.reshape(1, result.shape[0], -1) for result in out))  1.68 us

profile of v6, /device:TPU:1, one launch (start us, length us, event | category | flops | bytes accessed | tf_op | source)
XLA Modules:
  0.0 69.3 jit_solution(481382602846888062)
XLA Ops:
  1.3 64.4 %shard_map.156 = (bf16[128,1024]{1,0:T(8,128)(2,1)}, bf16[2,64,512]{2,1,0:T(8,128)(2,1)}, bf16[2,4096]{1,0:T(2,128)(2,1)}, bf16[2,256]{1,0:T(2,128)(2,1)}) custom-call(s32[1]{0:T(128)S(6)} %copy.20.length_ref, s32[1,8]{1,0:T(1,128)} %places_ref.1, f32[1,128]{1,0:T(1,128)} %constant.2.clone.frequency_ref, f32[1,512]{1,0:T(1,128)} %bitcast.18, ...), custom_call_target="tpu_custom_call" | custom-call | tf_op jit(solution)/shard_map/pallas_call | solution.py:667
  65.7 0.0 copy-start
  65.7 1.7 %reshape.25 = bf16[1,2,32768]{2,1,0:T(2,128)(2,1)} reshape(bf16[2,64,512]{2,1,0:T(8,128)(2,1)} %get-tuple-element.9) | data formatting | bytes 262144 | tf_op jit(solution)/shard_map/reshape | solution.py:736
  67.4 0.0 copy-done
  67.4 0.0 copy-start.1
  67.4 0.7 %copy.21 = bf16[1,128,1024]{2,1,0:T(8,128)(2,1)} copy(bf16[1,128,1024]{2,1,0:T(8,128)(2,1)S(1)} %bitcast.11) | data formatting | bytes 524288
  68.1 0.0 copy-done.1
  68.1 0.0 copy-start.2
  68.1 0.6 copy.22
  68.7 0.1 copy-done.2
  68.8 0.6 copy.23
Async XLA Ops:
  65.7 1.7 %copy-start = (bf16[128,1024]{1,0:T(8,128)(2,1)S(1)}, bf16[128,1024]{1,0:T(8,128)(2,1)}, u32[]{:S(2)}) copy-start(bf16[128,1024]{1,0:T(8,128)(2,1)} %get-tuple-element.8) | copy-start | bytes 786436
  67.4 0.7 %copy-start.1 = (bf16[2,4096]{1,0:T(2,128)(2,1)S(1)}, bf16[2,4096]{1,0:T(2,128)(2,1)}, u32[]{:S(2)}) copy-start(bf16[2,4096]{1,0:T(2,128)(2,1)} %get-tuple-element.10) | copy-start | bytes 49156
  68.1 0.7 copy-start.2

commit v7 on v1

--- a/solution.py
+++ b/solution.py
@@ -18,8 +18,7 @@
 NORM_EPS = 1e-06
 SCALE_EPS = 1e-06
 MASKED = -1e30
-FLOOR = -1e29
-FAR = 1 << 20
+FLOOR = -1e28
 
 
 def when(condition, action):
@@ -96,6 +95,7 @@
     chip_sum,
     group_part,
     keys,
+    marks,
     blocks,
     queries,
     total,
@@ -415,9 +415,20 @@
     loads[3].wait()
     loads[4].wait()
     keys[0, z, x, :, :lat] = pre_lat[...]
-    keys[0, z, x, :, lat:] = jnp.concatenate(
-        [pre_rope[...], jnp.zeros((PIECE, width - lat - rope), pre_rope.dtype)], axis=1
+    length = length_ref[0]
+    n_context = n_x * n_hi
+    piece_row = lax.broadcasted_iota(jnp.int32, (PIECE, width - lat), 0)
+    piece_lanes = lax.broadcasted_iota(jnp.int32, (PIECE, width - lat), 1)
+    pre_place = context * (n_lo * PIECE) + z_lo * PIECE + piece_row
+    hidden_key = jnp.logical_and(piece_lanes == rope + n_context, pre_place >= length)
+    pre_tail = jnp.concatenate(
+        [
+            pre_rope[...].astype(jnp.float32),
+            jnp.zeros((PIECE, width - lat - rope), jnp.float32),
+        ],
+        axis=1,
     )
+    keys[0, z, x, :, lat:] = jnp.where(hidden_key, MASKED, pre_tail).astype(jnp.bfloat16)
 
     pl.semaphore_wait(barrier, len(peers))
     ra_copy().start()
@@ -429,6 +440,20 @@
     loads[6].wait()
     loads[7].wait()
     lanes = lax.broadcasted_iota(jnp.int32, (tok, width - lat), 1)
+    later = jnp.logical_and(lanes > rope + context, lanes < rope + n_context)
+    masks = jnp.where(later, MASKED, jnp.where(lanes == rope + n_context, 1.0, 0.0))
+    key_row = lax.broadcasted_iota(jnp.int32, (tok, tok), 0)
+    query_lane = lax.broadcasted_iota(jnp.int32, (tok, tok), 1)
+    triangle = jnp.where(key_row > query_lane, MASKED, 0.0).astype(jnp.bfloat16)
+    marks[...] = jnp.zeros_like(marks)
+    mark_row = lax.broadcasted_iota(jnp.int32, (PIECE, tok), 0)
+    mark_lane = lax.broadcasted_iota(jnp.int32, (PIECE, tok), 1)
+    for place in range(n_lo):
+        for who in range(2):
+            first = (place * 2 + who) * PIECE
+            marks[1 + who, z_hi * n_lo + place, x] = jnp.where(
+                mark_lane == first + mark_row, 1.0, 0.0
+            ).astype(jnp.bfloat16)
 
     def absorb(first, last):
         for head in range(first, last):
@@ -443,7 +468,8 @@
             pair = pair.astype(jnp.float32)
             if head % 2:
                 pair = pltpu.roll(pair, rope, 1)
-            queries[lat:, columns] = jnp.where(lanes < rope, pair, 0.0).T.astype(jnp.bfloat16)
+            queries[lat:width, columns] = jnp.where(lanes < rope, pair, masks).T.astype(jnp.bfloat16)
+            queries[width:, columns] = triangle
 
     absorb(0, heads // 2)
 
@@ -456,15 +482,13 @@
         prefix_step(1)
     absorb(heads // 2, heads)
 
-    length = length_ref[0]
     position = (
         length
         + context * tok
         + tensor * PIECE
-        + lax.broadcasted_iota(jnp.int32, (PIECE, width - lat), 0)
+        + piece_row
     )
     sine, cosine = sine_cosine(position.astype(jnp.float32) * frequency_ref[...])
-    piece_lanes = lax.broadcasted_iota(jnp.int32, (PIECE, width - lat), 1)
     sine = jnp.where(piece_lanes < rope // 2, -sine, sine)
     sine = jnp.where(piece_lanes < rope, sine, 0.0)
 
@@ -488,7 +512,10 @@
         pltpu.roll(rope_sum, width - lat - rope // 2, 1),
         pltpu.roll(rope_sum, rope // 2, 1),
     )
-    keys[own_kind, z, x, :, lat:] = (rope_sum * cosine + swapped * sine).astype(jnp.bfloat16)
+    new_tail = rope_sum * cosine + swapped * sine
+    keys[own_kind, z, x, :, lat:] = jnp.where(
+        piece_lanes == rope + context, 1.0, new_tail
+    ).astype(jnp.bfloat16)
 
     for d in range(1, n_x):
         nx_copy(d).start()
@@ -512,26 +539,28 @@
 
     score_scale = float((nope + rope) ** (-0.5) * math.log2(math.e))
 
-    def attend(slots, spread, limit):
+    def attend(slots):
         block = n_x * PIECE
-        count = len(slots) * block
-        row = lax.broadcasted_iota(jnp.int32, (block, tok), 0)
-        within = lax.div(row, PIECE) * spread + lax.rem(row, PIECE)
-        bias = jnp.concatenate(
-            [jnp.where(within <= limit - start, 0.0, MASKED) for _, _, start in slots], axis=0
-        )
         key_rows = jnp.concatenate(
-            [keys[kind, place].reshape(block, width) for kind, place, _ in slots], axis=0
+            [
+                jnp.concatenate(
+                    [
+                        keys[kind, place].reshape(block, width),
+                        marks[kind, place].reshape(block, tok),
+                    ],
+                    axis=1,
+                )
+                for place in slots
+                for kind in range(3)
+            ],
+            axis=0,
         )
         latents = key_rows[:, :lat].T
         at_once = min(COLUMNS, heads * tok)
-        bias = jnp.concatenate([bias] * (at_once // tok), axis=1)
         for first in range(0, heads * tok, at_once):
             columns = pl.ds(first, at_once)
-            scores = jnp.dot(
-                key_rows, queries[:, columns], preferred_element_type=jnp.float32
-            )
-            scores = scores * score_scale + bias
+            scores = jnp.dot(key_rows, queries[:, columns], preferred_element_type=jnp.float32)
+            scores = scores * score_scale
             old_top = top[:, columns]
             new_top = jnp.maximum(old_top, jnp.max(scores, axis=0, keepdims=True))
             top[:, columns] = new_top
@@ -544,18 +573,6 @@
                 latents, exponents.astype(jnp.bfloat16), preferred_element_type=jnp.float32
             )
 
-    pre_dev = n_lo * PIECE
-
-    def prefix_slot(place):
-        return (0, place, lax.div(place, n_lo) * pre_dev + lax.rem(place, n_lo) * PIECE)
-
-    def new_slot(kind, place, push=0):
-        start = lax.div(place, n_lo) * tok + lax.rem(place, n_lo) * 2 * PIECE
-        return (kind, place, start + (kind - 1) * PIECE + push)
-
-    prefix_limit = length - 1
-    new_limit = context * tok + lax.broadcasted_iota(jnp.int32, (n_x * PIECE, tok), 1)
-
     def iteration(s, carry):
         new_step(s)
         prefix_step(s + 3)
@@ -581,39 +598,14 @@
 
         pl.when(s == half)(owners_done)
 
-        def attend_prefix():
-            last = jnp.where(s + 1 == half, z, wrap(z - (s + 1)))
-            attend(
-                [
-                    prefix_slot(wrap(z - s)),
-                    prefix_slot(wrap(z + s)),
-                    prefix_slot(wrap(z + s + 1)),
-                    prefix_slot(last),
-                ],
-                n_hi * pre_dev,
-                prefix_limit,
-            )
-
-        pl.when(lax.rem(s, 2) == 1)(attend_prefix)
-        push = jnp.where(s == 1, FAR, 0)
-        before, after = wrap(z - (s - 1)), wrap(z + (s - 1))
-        attend(
-            [
-                new_slot(1, before),
-                new_slot(2, before),
-                new_slot(1, after, push),
-                new_slot(2, after, push),
-            ],
-            n_hi * tok,
-            new_limit,
-        )
+        pl.when(s > 1)(lambda: attend([wrap(z - (s - 1)), wrap(z + (s - 1))]))
         return carry
 
+    attend([z])
     lax.fori_loop(1, half + 1, iteration, 0)
     for kind in (1, 2):
         nd_last_arrival(kind).wait_recv()
-    far = wrap(z + half)
-    attend([new_slot(1, far), new_slot(2, far)], n_hi * tok, new_limit)
+    attend([wrap(z + half)])
 
     loads[8].wait()
     for head in range(heads):
@@ -762,8 +754,9 @@
             pltpu.VMEM((n_lo, PIECE, width), f32),
             pltpu.VMEM((max(n_lo - 1, 1), PIECE, width), f32),
             pltpu.VMEM((3, n_z, n_x, PIECE, width), bf16),
+            pltpu.VMEM((3, n_z, n_x, PIECE, tok), bf16),
             pltpu.VMEM((2, n_rep * n_lo, PIECE, width), bf16),
-            pltpu.VMEM((width, heads * tok), bf16),
+            pltpu.VMEM((width + tok, heads * tok), bf16),
             pltpu.VMEM((lat, heads * tok), f32),
             pltpu.VMEM((1, heads * tok), f32),
             pltpu.VMEM((1, heads * tok), f32),

time: 67.4 us -> 66 us (0.979)
  Pallas kernels: 62.2 us -> 60.8 us
    pallas_call x1, Pallas kernels: 62.2 us -> 60.8 us  [per_device(): pl.pallas_call(functools.partial(kernel, shape), out_shape=(jax.ShapeDtyp...]
where the time goes in v7:
time: 66 us; the launch traced here: 65.8 us
  Pallas kernels  60.8 us (92%)
  local copies, waits for them, and re-layouts  3.67 us (6%)
  between operations  1.3 us (2%)
    pallas_call x1, Pallas kernels, per_device(): pl.pallas_call(functools.partial(kernel, shape), out_shape=(jax.ShapeDtyp...  60.8 us
    unnamed x10, local copies, waits for them, and re-layouts  3.67 us

profile of v7, /device:TPU:1, one launch (start us, length us, event | category | flops | bytes accessed | tf_op | source)
XLA Modules:
  0.0 65.8 jit_solution(2922223089158158424)
XLA Ops:
  1.3 60.8 %shard_map.156 = (bf16[128,1024]{1,0:T(8,128)(2,1)}, bf16[2,32768]{1,0:T(2,128)(2,1)}, bf16[2,4096]{1,0:T(2,128)(2,1)}, bf16[2,256]{1,0:T(2,128)(2,1)}) custom-call(s32[1]{0:T(128)S(6)} %copy.21.length_ref, s32[1,8]{1,0:T(1,128)} %places_ref.1, f32[1,128]{1,0:T(1,128)} %constant.2.clone.frequency_ref, f32[1,512]{1,0:T(1,128)} %bitcast.20, ...), custom_call_target="tpu_custom_call" | custom-call | tf_op jit(solution)/shard_map/pallas_call | solution.py:732
  62.1 0.0 copy-start
  62.1 1.7 %copy.22 = bf16[1,128,1024]{2,1,0:T(8,128)(2,1)} copy(bf16[1,128,1024]{2,1,0:T(8,128)(2,1)} %bitcast.12) | data formatting | bytes 524288
  63.8 0.0 copy-done
  63.8 0.0 copy-start.1
  63.8 0.7 copy.23
  64.5 0.1 copy-done.1
  64.5 0.0 copy-start.2
  64.5 0.6 copy.24
  65.1 0.1 copy-done.2
  65.2 0.6 copy.25
Async XLA Ops:
  62.1 1.7 %copy-start = (bf16[2,32768]{1,0:T(2,128)(2,1)S(1)}, bf16[2,32768]{1,0:T(2,128)(2,1)}, u32[]{:S(2)}) copy-start(bf16[2,32768]{1,0:T(2,128)(2,1)} %get-tuple-element.9) | copy-start | bytes 393220
  63.8 0.7 %copy-start.1 = (bf16[2,4096]{1,0:T(2,128)(2,1)S(1)}, bf16[2,4096]{1,0:T(2,128)(2,1)}, u32[]{:S(2)}) copy-start(bf16[2,4096]{1,0:T(2,128)(2,1)} %get-tuple-element.10) | copy-start | bytes 49156
  64.5 0.7 %copy-start.2 = (bf16[2,256]{1,0:T(2,128)(2,1)S(1)}, bf16[2,256]{1,0:T(2,128)(2,1)}, u32[]{:S(2)}) copy-start(bf16[2,256]{1,0:T(2,128)(2,1)} %get-tuple-element.11) | copy-start | bytes 3076

commit v8 on v7

--- a/solution.py
+++ b/solution.py
@@ -436,6 +436,11 @@
     for d in range(1, n_x):
         px_copy(0, d).start()
 
+    ra_copy().wait_recv()
+    chip_sum[...] = partial[core] + partner_part[...]
+    for d in range(1, n_lo):
+        rb_copy(d).start()
+
     loads[5].wait()
     loads[6].wait()
     loads[7].wait()
@@ -472,11 +477,6 @@
             queries[width:, columns] = triangle
 
     absorb(0, heads // 2)
-
-    ra_copy().wait_recv()
-    chip_sum[...] = partial[core] + partner_part[...]
-    for d in range(1, n_lo):
-        rb_copy(d).start()
 
     if half >= 1:
         prefix_step(1)
@@ -598,10 +598,10 @@
 
         pl.when(s == half)(owners_done)
 
+        pl.when(s == 1)(lambda: attend([z]))
         pl.when(s > 1)(lambda: attend([wrap(z - (s - 1)), wrap(z + (s - 1))]))
         return carry
 
-    attend([z])
     lax.fori_loop(1, half + 1, iteration, 0)
     for kind in (1, 2):
         nd_last_arrival(kind).wait_recv()

time: 66 us -> 66 us (level)
  no operation moved by 1% of the time
where the time goes in v8:
time: 66 us; the launch traced here: 65.8 us
  Pallas kernels  60.8 us (92%)
  local copies, waits for them, and re-layouts  3.67 us (6%)
  between operations  1.3 us (2%)
    pallas_call x1, Pallas kernels, per_device(): pl.pallas_call(functools.partial(kernel, shape), out_shape=(jax.ShapeDtyp...  60.8 us
    unnamed x10, local copies, waits for them, and re-layouts  3.67 us

profile of v8, /device:TPU:1, one launch (start us, length us, event | category | flops | bytes accessed | tf_op | source)
XLA Modules:
  0.0 65.8 jit_solution(17246055549763458953)
XLA Ops:
  1.3 60.8 %shard_map.156 = (bf16[128,1024]{1,0:T(8,128)(2,1)}, bf16[2,32768]{1,0:T(2,128)(2,1)}, bf16[2,4096]{1,0:T(2,128)(2,1)}, bf16[2,256]{1,0:T(2,128)(2,1)}) custom-call(s32[1]{0:T(128)S(6)} %copy.21.length_ref, s32[1,8]{1,0:T(1,128)} %places_ref.1, f32[1,128]{1,0:T(1,128)} %constant.2.clone.frequency_ref, f32[1,512]{1,0:T(1,128)} %bitcast.20, ...), custom_call_target="tpu_custom_call" | custom-call | tf_op jit(solution)/shard_map/pallas_call | solution.py:732
  62.1 0.0 copy-start
  62.1 1.7 %copy.22 = bf16[1,128,1024]{2,1,0:T(8,128)(2,1)} copy(bf16[1,128,1024]{2,1,0:T(8,128)(2,1)} %bitcast.12) | data formatting | bytes 524288
  63.8 0.0 copy-done
  63.8 0.0 copy-start.1
  63.8 0.7 copy.23
  64.5 0.1 copy-done.1
  64.5 0.0 copy-start.2
  64.5 0.6 copy.24
  65.1 0.1 copy-done.2
  65.2 0.6 copy.25
Async XLA Ops:
  62.1 1.7 %copy-start = (bf16[2,32768]{1,0:T(2,128)(2,1)S(1)}, bf16[2,32768]{1,0:T(2,128)(2,1)}, u32[]{:S(2)}) copy-start(bf16[2,32768]{1,0:T(2,128)(2,1)} %get-tuple-element.9) | copy-start | bytes 393220
  63.8 0.7 %copy-start.1 = (bf16[2,4096]{1,0:T(2,128)(2,1)S(1)}, bf16[2,4096]{1,0:T(2,128)(2,1)}, u32[]{:S(2)}) copy-start(bf16[2,4096]{1,0:T(2,128)(2,1)} %get-tuple-element.10) | copy-start | bytes 49156
  64.5 0.7 %copy-start.2 = (bf16[2,256]{1,0:T(2,128)(2,1)S(1)}, bf16[2,256]{1,0:T(2,128)(2,1)}, u32[]{:S(2)}) copy-start(bf16[2,256]{1,0:T(2,128)(2,1)} %get-tuple-element.11) | copy-start | bytes 3076
